TPU v7x, 128 devices: a whole 4x4x4 slice. The times are simulated.
128 devices in a mesh: gx: 4 (over y), gy: 32 (over x, z, core).
Axes of the slice: x: 4, y: 4, z: 4, core: 2. Of those that a mesh axis runs over, the one named last changes fastest.
Arguments:
- blocks: float32 [4, 32, 2, 4, 23, 828], P('gx', 'gy'), may hold values from -1.5 to 1.5, as said below
- halo_members: int32 [4, 32, 28], P('gx', 'gy'), may hold values from -1 to 35, as said below
- chem_potential: float32 [1], replicated, may hold values from -0.8 to 0.8
Outputs:
- density: float32 [4, 32, 4, 23, 828], P('gx', 'gy')
Inputs may be any that keep to these rules, and one draw needn't show every extreme that they name: `blocks`: index 0 of the third dimension holds margin rows, index 1 Kohn-Sham rows; every assembled margin submatrix is positive definite. `halo_members`: per device, the used slots come first and hold distinct codes t * 4 + b with t != 4; the rest are -1; at least 14 are used.
All inputs are finite; a program needn't handle non-finite values.
Results may differ from a plain program's by a relative error of at most 0.0003.
Values sent between devices are 32-bit elements; how exact they have to be, the bound alone decides.
No kernel may reach another device: no remote copies, remote signals or barrier semaphores. Data moves between devices by JAX's collectives and lax.ppermute only.
A program may use at most 192 MiB of HBM per device.

v0:
```python
import functools

import jax
import jax.numpy as jnp
from jax import lax
from jax.experimental import pallas as pl
from jax.experimental.pallas import tpu as pltpu
from jax.sharding import PartitionSpec as P

F = 23
G = 24
SUBMOL = 32
MT = 4
TILE = MT * F
DIM = SUBMOL * G
ROWS = MT * G
CODES = 9 * MT
WIDE = 9 * TILE
LANES = 896
EDGE = 640
SIDE = 1152
CORNER = 768
NEAR = 640
ZERO = 840
B = 256
f32 = jnp.float32
bf16 = jnp.bfloat16
VMEM = pl.BlockSpec(memory_space=pltpu.VMEM)
SMEM = pl.BlockSpec(memory_space=pltpu.SMEM)
LIMIT = 32 * 2**20


def params():
    return pltpu.CompilerParams(vmem_limit_bytes=LIMIT)


def dot(a, b):
    return jnp.dot(a, b, preferred_element_type=f32)


def halves(x):
    hi = x.astype(bf16)
    return hi, (x - hi.astype(f32)).astype(bf16)


def fold(v, ref):
    whole = ref.shape[1]
    rest = v.shape[1] - whole
    each = 12 * 128 // whole
    parts = []
    for g in range(12):
        parts.append(v[8 * g : 8 * (g + 1), whole:])
        if (g + 1) % each == 0:
            parts.append(jnp.zeros((8, 128 - each * rest), f32))
    ref[:ROWS] = v[:, :whole]
    ref[ROWS:] = jnp.concatenate(parts, axis=1)


def unfold(ref, rest):
    each = 12 * 128 // ref.shape[1]
    starts = [128 * (g // each) + rest * (g % each) for g in range(12)]
    last = jnp.concatenate([ref[ROWS : ROWS + 8, a : a + rest] for a in starts], axis=0)
    return jnp.concatenate([ref[:ROWS], last], axis=1)


def pack_kernel(q, blocks_ref, down_ref, up_ref, own_ref, held, sems):
    cuts = (0, 6, 12, 18, F)
    copies = []
    for n in range(4):
        f = pl.ds(cuts[n], cuts[n + 1] - cuts[n])
        copies.append(pltpu.make_async_copy(blocks_ref.at[q, f], held.at[f], sems.at[n]))
    for copy in copies:
        copy.start()
    for copy in copies:
        copy.wait()
    parts = [held[f] for f in range(F)] + [jnp.zeros((MT, WIDE), f32)]
    own = jnp.concatenate(parts, axis=0)
    own_ref[:, :WIDE] = own
    own_ref[:, WIDE:] = jnp.zeros((ROWS, LANES - WIDE), f32)
    down_ref[...] = own[:, :EDGE]
    up_ref[...] = jnp.concatenate([own[:, 276:], blank(EDGE - 552)], axis=1)


def blank(width):
    return jnp.zeros((ROWS, width), f32)


def side_kernel(odd_ref, margin_ref, ham_ref, cross_ref):
    def packed(o):
        parts = [ref[:, 276 * n + o : 276 * n + o + 184] for ref in (margin_ref, ham_ref) for n in range(3)]
        return jnp.concatenate(parts + [blank(SIDE - 6 * 184)], axis=1)

    cross_ref[...] = jnp.where(odd_ref[0] == 1, packed(TILE), packed(0))


def corner_kernel(odd_ref, own_ref, plus_ref, minus_ref, cross_ref, inner_ref, near_ref):
    rows = (plus_ref[:, :552], minus_ref[:, :552])
    own = own_ref[...]

    def packed(o):
        parts = [v[:, 276 * n + o : 276 * n + o + 184] for v in rows for n in range(2)]
        return jnp.concatenate(parts + [blank(CORNER - 184 * 4)], axis=1)

    def near(o):
        parts = [own[:, 276 * n + o : 276 * n + o + 184] for n in range(3)]
        return jnp.concatenate(parts + [blank(NEAR - 184 * 3)], axis=1)

    odd = odd_ref[0] == 1
    to_plus, to_minus = packed(TILE), packed(0)
    cross_ref[...] = jnp.where(odd, to_plus, to_minus)
    inner_ref[...] = jnp.where(odd, to_minus, to_plus)
    near_ref[...] = jnp.where(odd, near(0), near(TILE))


def put(block, at, hi_ref, lo_ref):
    hi = block.astype(bf16)
    hi_ref[at] = hi
    lo_ref[at] = (block - hi.astype(f32)).astype(bf16)


def diagonal(rows, shift):
    row = lax.broadcasted_iota(jnp.int32, (rows, B), 0)
    return row == lax.broadcasted_iota(jnp.int32, (rows, B), 1) + shift


def part(i):
    return slice(B * i, B * (i + 1))


def column_sums(matrix):
    return jnp.sum(jnp.abs(matrix), axis=0, keepdims=True)


def largest(sums):
    return jnp.max(jnp.maximum(jnp.maximum(sums[0], sums[1]), sums[2]))


def assemble(q, odd_ref, codes_ref, own_ref, plus_ref, minus_ref, side_ref, cross_ref, inner_ref, near_ref, work, unit, sink):
    rows, picked, cols = work

    def set_rows(t, v):
        for c in range(LANES // 128):
            rows[c, t * ROWS : (t + 1) * ROWS] = v[:, 128 * c : 128 * (c + 1)]

    set_rows(4, own_ref[...])
    set_rows(7, jnp.concatenate([blank(276), plus_ref[:, :552], blank(LANES - 828)], axis=1))
    set_rows(1, jnp.concatenate([minus_ref[:, :552], blank(LANES - 552)], axis=1))
    set_rows(9, blank(LANES))

    def place(side_ref, begin, corner_ref, ahead):
        gap = TILE * ahead
        for base, ref, first, count, left in (
            (3, side_ref, begin, 3, 0), (6, corner_ref, 0, 2, 276), (0, corner_ref, 368, 2, 0),
        ):
            parts = [blank(left + gap)] if left + gap else []
            for n in range(count):
                parts += [ref[:, first + 184 * n : first + 184 * (n + 1)], blank(TILE)]
            parts[-1] = blank(LANES - left - gap - 276 * count + TILE)
            set_rows(base + 2 * ahead, jnp.concatenate(parts, axis=1))

    @pl.when(odd_ref[0] == 1)
    def _():
        place(side_ref, 552 * q, cross_ref, 1)
        place(near_ref, 0, inner_ref, 0)

    @pl.when(odd_ref[0] != 1)
    def _():
        place(side_ref, 552 * q, cross_ref, 0)
        place(near_ref, 0, inner_ref, 1)

    codes = [codes_ref[k] for k in range(SUBMOL)]
    begin = [jnp.where(c >= 0, (c >> 2) * ROWS + (c & 3), 9 * ROWS) for c in codes]
    for c in range(LANES // 128):
        for h in range(2):
            slots = range(16 * h, 16 * (h + 1))
            turned = jnp.concatenate([rows[c, pl.ds(begin[k], G, stride=MT)] for k in slots], axis=0).T
            for j in range(3):
                cols[3 * h + j, 128 * c : 128 * (c + 1)] = turned[:, 128 * j : 128 * (j + 1)]
    begin = [jnp.where(c >= 0, c * F, ZERO) for c in codes]
    row = lax.broadcasted_iota(jnp.int32, (8, 128), 0)
    lane = lax.broadcasted_iota(jnp.int32, (G, 128), 1)
    line = lax.broadcasted_iota(jnp.int32, (G, 128), 0)
    for k in range(SUBMOL):
        for j in range(DIM // 128):
            block = cols[j, pl.ds(begin[k], G)]
            block = jnp.concatenate([block[:16], jnp.where(row < 7, block[16:], 0.0)], axis=0)
            if unit and G * k < 128 * (j + 1) and G * (k + 1) > 128 * j:
                ones = jnp.where(lane + 128 * j == line + G * k, 1.0, 0.0)
                block = jnp.where(codes[k] >= 0, block, ones)
            picked[k * G : (k + 1) * G, 128 * j : 128 * (j + 1)] = block
    for i in range(3):
        for j in range(i, 3):
            sink(i, j, 0.5 * (picked[part(i), part(j)] + picked[part(j), part(i)].T))


def symmetric_product(ah, al, bh, bl, sink):
    for j in range(3):
        c = part(j)
        r = B * (j + 1)
        block = dot(ah[:r], bh[:, c]) + dot(ah[:r], bl[:, c]) + dot(al[:r], bh[:, c])
        for i in range(j + 1):
            sink(i, j, block[part(i)])


def put_both(i, j, block, hi_ref, lo_ref):
    put(block, (part(i), part(j)), hi_ref, lo_ref)
    if i < j:
        put(block.T, (part(j), part(i)), hi_ref, lo_ref)


def root_kernel(
    odd_ref, codes_ref, own_ref, plus_ref, minus_ref, side_ref, cross_ref, inner_ref, near_ref,
    margin_ref, root_hi, root_lo, rows, picked, cols, hi, lo, hi2, lo2,
):
    sums = [jnp.zeros((1, B), f32)] * 3

    def first(i, j, block):
        margin_ref[part(i), part(j)] = block
        put_both(i, j, block, hi, lo)
        sums[j] += column_sums(block)
        if i < j:
            other = block.T
            margin_ref[part(j), part(i)] = other
            sums[i] += column_sums(other)

    assemble(
        0, odd_ref, codes_ref, own_ref, plus_ref, minus_ref, side_ref, cross_ref, inner_ref, near_ref,
        (rows, picked, cols), True, first,
    )
    bound = largest(sums)
    one = 1.0 / jnp.full((1, B), bound, f32)
    two = one * one
    root = lax.rsqrt(jnp.full((1, B), bound, f32)) * 0.0625

    def second(i, j, block):
        value = block * two - (4.5 * one) * margin_ref[part(i), part(j)]
        if i == j:
            value = value + jnp.where(diagonal(B, 0), 3.375, 0.0)
        put_both(i, j, value, hi2, lo2)

    symmetric_product(hi, lo, hi, lo, second)

    def third(i, j, block):
        value = block - (8.625 * one) * margin_ref[part(i), part(j)]
        if i == j:
            value = value + jnp.where(diagonal(B, 0), 24.609375, 0.0)
        put_both(i, j, value * root, root_hi, root_lo)

    symmetric_product(hi2, lo2, hi2, lo2, third)


def density_kernel(
    odd_ref, codes_ref, chem_ref, own_ref, plus_ref, minus_ref, side_ref, cross_ref, inner_ref, near_ref,
    margin_ref, root_hi, root_lo, spread, up_ref, mid_ref, down_ref,
    rows, picked, cols, hi, lo, hi2, lo2, hi3, lo3, narrow, tall, pieces,
):
    chem = chem_ref[0]

    def first(i, j, block):
        put_both(i, j, block - chem * margin_ref[part(i), part(j)], hi, lo)

    assemble(
        1, odd_ref, codes_ref, own_ref, plus_ref, minus_ref, side_ref, cross_ref, inner_ref, near_ref,
        (rows, picked, cols), False, first,
    )
    for j in range(3):
        c = part(j)
        half = dot(root_hi[...], hi[:, c]) + dot(root_hi[...], lo[:, c]) + dot(root_lo[...], hi[:, c])
        put(half, (slice(None), c), hi2, lo2)
    sums = [jnp.zeros((1, B), f32)] * 3

    def second(i, j, block):
        put(block, (part(i), part(j)), hi, lo)
        sums[j] += column_sums(block)
        if i < j:
            other = block.T
            put(other, (part(j), part(i)), hi, lo)
            sums[i] += column_sums(other)

    symmetric_product(hi2, lo2, root_hi, root_lo, second)
    scale = 1.0 / jnp.full((1, B), largest(sums) + 1e-06, f32)
    half_two = 0.5 * (scale * scale)

    def third(i, j, block):
        value = -half_two * block
        if i == j:
            value = value + jnp.where(diagonal(B, 0), 1.5, 0.0)
        put_both(i, j, value, hi2, lo2)

    symmetric_product(hi, lo, hi, lo, third)

    def fourth(i, j, block):
        put_both(i, j, block * scale, hi3, lo3)

    symmetric_product(hi, lo, hi2, lo2, fourth)

    def thin(v, bh, bl):
        vh, vl = halves(v)
        both = jnp.concatenate([vh, vl], axis=0)
        whole = dot(both, bh[...])
        return whole[:ROWS] + whole[ROWS:] + dot(vh, bl[...])

    def once(v):
        return thin(v, hi3, lo3)

    def next_sign(v):
        return once(1.5 * v - 0.5 * once(once(v)))

    core = root_hi[:ROWS].astype(f32) + root_lo[:ROWS].astype(f32)
    inside = 1.5 * core - 0.5 * next_sign(next_sign(core))
    density = thin(core - next_sign(inside), root_hi, root_lo)

    narrow[...] = jnp.zeros((128, DIM), f32)
    for m in range(MT):
        narrow[m * F : (m + 1) * F] = density[m * G : m * G + F]
    for j in range(DIM // 128):
        tall[128 * j : 128 * (j + 1)] = narrow[:, 128 * j : 128 * (j + 1)].T
    spread[...] = jnp.zeros((CODES * G, 128), f32)
    for k in range(SUBMOL):
        code = codes_ref[k]

        @pl.when(code >= 0)
        def _():
            spread[pl.ds(pl.multiple_of(code * G, 8), G)] = tall[k * G : (k + 1) * G]

    odd = odd_ref[0]
    for dx, ref in ((-1, down_ref), (0, mid_ref), (1, up_ref)):
        for dy in (-1, 0, 1):
            place = 1 + dy - 2 * dy * odd
            t = 3 * (dx + 1) + dy + 1
            for m in range(MT):
                block = spread[t * ROWS + m * G : t * ROWS + m * G + F]
                pieces[place, pl.ds(m, F, stride=MT)] = block
            pieces[place, MT * F :] = jnp.zeros((ROWS - MT * F, 128), f32)
        v = jnp.concatenate([pieces[n][:, :TILE] for n in range(3)], axis=1)
        if dx:
            fold(v, ref)
        else:
            ref[...] = v


def own_kernel(spread, w_ref, flat):
    for c in range(CODES):
        flat[c * F : c * F + G] = spread[c * G : (c + 1) * G]
    flat[WIDE:LANES] = jnp.zeros((LANES - WIDE, 128), f32)
    for c in range(LANES // 128):
        own = flat[128 * c : 128 * (c + 1)].T
        for m in range(MT):
            w_ref[c, pl.ds(m, F, stride=MT)] = own[m * F : (m + 1) * F]
        w_ref[c, MT * F :] = jnp.zeros((ROWS - MT * F, 128), f32)


def turn_kernel(mid_ref, up_ref, down_ref, cross_ref, inner_ref):
    rows = (mid_ref[...], unfold(up_ref, 20), unfold(down_ref, 20))
    fold(jnp.concatenate([v[:, :TILE] for v in rows], axis=1), cross_ref)
    fold(jnp.concatenate([v[:, 2 * TILE :] for v in rows], axis=1), inner_ref)


def final_kernel(odd_ref, w_ref, mid_ref, up_ref, down_ref, cross_ref, inner_ref, out_ref):
    odd = odd_ref[0] == 1
    cross, inner = unfold(cross_ref, 20), unfold(inner_ref, 20)
    plus = jnp.where(odd, cross, inner)
    minus = jnp.where(odd, inner, cross)
    middle = (mid_ref[...], unfold(up_ref, 20), unfold(down_ref, 20))
    parts = []
    for n in (1, 0, 2):
        parts += [v[:, TILE * k : TILE * (k + 1)] for v, k in ((minus, n), (middle[n], 1), (plus, n))]
    received = jnp.concatenate(parts, axis=1)
    own = jnp.concatenate([w_ref[c] for c in range(LANES // 128)], axis=1)
    whole = 0.5 * (own[: MT * F, :WIDE] + received[: MT * F])
    for g in range(F):
        out_ref[g] = whole[MT * g : MT * (g + 1)]


def struct(shape, dtype=f32):
    return jax.ShapeDtypeStruct(shape, dtype)


def shards(blocks, halo_members, chem_potential):
    n_x, n_y = lax.axis_size("gx"), lax.axis_size("gy")
    ahead = [(i, (i + 1) % n_x) for i in range(n_x)]
    back = [((i + 1) % n_x, i) for i in range(n_x)]
    crossing = [(j, (j + 1) % n_y if j % 2 else (j - 1) % n_y) for j in range(n_y)]
    inside = [(j, j ^ 1) for j in range(n_y)]
    odd = (lax.axis_index("gy") % 2).astype(jnp.int32).reshape(1)
    codes = jnp.concatenate([4 * MT + jnp.arange(MT, dtype=jnp.int32), halo_members[0, 0]])
    ANY = pl.BlockSpec(memory_space=pltpu.HBM)
    native = pltpu.with_memory_space_constraint(jnp.transpose(blocks[0, 0], (0, 2, 1, 3)), pltpu.HBM)

    plus, minus, own = [], [], []
    for q in range(2):
        down, up, mine = pl.pallas_call(
            functools.partial(pack_kernel, q),
            out_shape=[struct((ROWS, EDGE)), struct((ROWS, EDGE)), struct((ROWS, LANES))],
            in_specs=[ANY],
            out_specs=[VMEM] * 3,
            scratch_shapes=[pltpu.VMEM((F, MT, WIDE), f32), pltpu.SemaphoreType.DMA((4,))],
            name=f"pack{q}",
            compiler_params=params(),
        )(native)
        plus.append(lax.ppermute(down, "gx", back))
        minus.append(lax.ppermute(up, "gx", ahead))
        own.append(mine)
    side = pl.pallas_call(
        side_kernel,
        out_shape=struct((ROWS, SIDE)),
        in_specs=[SMEM, VMEM, VMEM],
        out_specs=VMEM,
        name="side",
        compiler_params=params(),
    )(odd, *own)
    side = lax.ppermute(side, "gy", crossing)
    corners = []
    for q in range(2):
        x, i, near = pl.pallas_call(
            corner_kernel,
            out_shape=[struct((ROWS, CORNER)), struct((ROWS, CORNER)), struct((ROWS, NEAR))],
            in_specs=[SMEM, VMEM, VMEM, VMEM],
            out_specs=[VMEM] * 3,
            name=f"corner{q}",
            compiler_params=params(),
            cost_estimate=pl.CostEstimate(flops=(0, 40000000000)[q], bytes_accessed=(1, 10**8)[q], transcendentals=0),
        )(odd, own[q], plus[q], minus[q])
        corners.append(
            (lax.ppermute(x, "gy", crossing), lax.ppermute(i, "gy", inside), lax.ppermute(near, "gy", inside))
        )
    square = pltpu.VMEM((DIM, DIM), bf16)
    work = [
        pltpu.VMEM((LANES // 128, 10 * ROWS, 128), f32),
        pltpu.VMEM((DIM, DIM), f32),
        pltpu.VMEM((DIM // 128, LANES, 128), f32),
    ]
    margin, root_hi, root_lo = pl.pallas_call(
        root_kernel,
        out_shape=[struct((DIM, DIM)), struct((DIM, DIM), bf16), struct((DIM, DIM), bf16)],
        in_specs=[SMEM, SMEM] + [VMEM] * 7,
        out_specs=[VMEM] * 3,
        scratch_shapes=work + [square] * 4,
        name="inverse_root",
        compiler_params=params(),
        cost_estimate=pl.CostEstimate(flops=4 * 2 * DIM**3, bytes_accessed=2**23, transcendentals=0),
    )(odd, codes, own[0], plus[0], minus[0], side, *corners[0])
    folded = struct((ROWS + 8, 256))
    spread, up, mid, down = pl.pallas_call(
        density_kernel,
        out_shape=[struct((CODES * G, 128)), folded, struct((ROWS, 3 * TILE)), folded],
        in_specs=[SMEM, SMEM, SMEM] + [VMEM] * 10,
        out_specs=[VMEM] * 4,
        scratch_shapes=work
        + [square] * 6
        + [pltpu.VMEM((128, DIM), f32), pltpu.VMEM((DIM, 128), f32), pltpu.VMEM((3, ROWS, 128), f32)],
        name="density",
        compiler_params=params(),
        cost_estimate=pl.CostEstimate(flops=12 * 2 * DIM**3, bytes_accessed=2**23, transcendentals=0),
    )(odd, codes, chem_potential, own[1], plus[1], minus[1], side, *corners[1], margin, root_hi, root_lo)
    from_minus = lax.ppermute(up, "gx", ahead)
    from_plus = lax.ppermute(down, "gx", back)
    w = pl.pallas_call(
        own_kernel,
        out_shape=struct((LANES // 128, ROWS, 128)),
        in_specs=[VMEM],
        out_specs=VMEM,
        scratch_shapes=[pltpu.VMEM((LANES, 128), f32)],
        name="own",
        compiler_params=params(),
    )(spread)
    x, i = pl.pallas_call(
        turn_kernel,
        out_shape=[folded] * 2,
        in_specs=[VMEM] * 3,
        out_specs=[VMEM] * 2,
        name="turn",
        compiler_params=params(),
    )(mid, from_minus, from_plus)
    x = lax.ppermute(x, "gy", crossing)
    i = lax.ppermute(i, "gy", inside)
    out = pl.pallas_call(
        final_kernel,
        out_shape=struct((F, MT, WIDE)),
        in_specs=[SMEM] + [VMEM] * 6,
        out_specs=VMEM,
        name="symmetrize",
        compiler_params=params(),
    )(odd, w, mid, from_minus, from_plus, x, i)
    return jnp.transpose(out, (1, 0, 2))[None, None]


def solution(mesh):
    return jax.shard_map(
        shards,
        mesh=mesh,
        in_specs=(P("gx", "gy", None, None, None, None), P("gx", "gy", None), P()),
        out_specs=P("gx", "gy", None, None, None),
        check_vma=False,
    )
```

profile of v0, /device:TPU:24, one launch (start us, length us, event | category | flops | bytes accessed | tf_op | source)
XLA Modules:
  0.0 64.8 jit_solution(894999975037734326)
XLA Ops:
  0.0 1.2 %pack0.1 = (f32[96,640]{1,0:T(8,128)S(1)}, f32[96,640]{1,0:T(8,128)S(1)}, f32[96,896]{1,0:T(8,128)S(1)}) custom-call(f32[2,23,4,828]{3,2,1,0:T(4,128)} %bitcast.8), custom_call_target="tpu_custom_call" | custom-call | tf_op jit(solution)/shard_map/pack0/pallas_call | solution.py:392
  1.2 0.8 %collective-permute-start.6 = (f32[96,640]{1,0:T(8,128)S(1)}, f32[96,640]{1,0:T(8,128)S(1)}, u32[]{:S(2)}, u32[]{:S(2)}) collective-permute-start(f32[96,640]{1,0:T(8,128)S(1)} %get-tuple-element.33), channel_id=1, source_target_pairs={{32,0},{64,32},{96,64},{0,96},{33,1},{65,33},{97,65},{1,97},{34,2}... | collective-permute-start | bytes 737288 | tf_op jit(solution)/shard_map/ppermute | solution.py:401
  2.0 2.5 %collective-permute-start.7 = (f32[96,640]{1,0:T(8,128)S(1)}, f32[96,640]{1,0:T(8,128)S(1)}, u32[]{:S(2)}, u32[]{:S(2)}) collective-permute-start(f32[96,640]{1,0:T(8,128)S(1)} %get-tuple-element.34), channel_id=1, source_target_pairs={{0,32},{32,64},{64,96},{96,0},{1,33},{33,65},{65,97},{97,1},{2,34}... | collective-permute-start | bytes 737288 | tf_op jit(solution)/shard_map/ppermute | solution.py:402
  4.5 1.2 %pack1.1 = (f32[96,640]{1,0:T(8,128)S(1)}, f32[96,640]{1,0:T(8,128)S(1)}, f32[96,896]{1,0:T(8,128)S(1)}) custom-call(f32[2,23,4,828]{3,2,1,0:T(4,128)} %bitcast.9), custom_call_target="tpu_custom_call" | custom-call | tf_op jit(solution)/shard_map/pack1/pallas_call | solution.py:392
  5.7 0.1 collective-permute-start
  5.8 3.2 %collective-permute-start.1 = (f32[96,640]{1,0:T(8,128)S(1)}, f32[96,640]{1,0:T(8,128)S(1)}, u32[]{:S(2)}, u32[]{:S(2)}) collective-permute-start(f32[96,640]{1,0:T(8,128)S(1)} %get-tuple-element.28), channel_id=1, source_target_pairs={{0,32},{32,64},{64,96},{96,0},{1,33},{33,65},{65,97},{97,1},{2,34}... | collective-permute-start | bytes 737288 | tf_op jit(solution)/shard_map/ppermute | solution.py:402
  9.0 0.3 side.1
  9.4 4.6 %collective-permute-start.2 = (f32[96,1152]{1,0:T(8,128)S(1)}, f32[96,1152]{1,0:T(8,128)S(1)}, u32[]{:S(2)}, u32[]{:S(2)}) collective-permute-start(f32[96,1152]{1,0:T(8,128)S(1)} %side.1), channel_id=1, source_target_pairs={{0,31},{1,2},{2,1},{3,4},{4,3},{5,6},{6,5},{7,8},{8,7},{9,10},{10,... | collective-permute-start | bytes 1327112 | tf_op jit(solution)/shard_map/ppermute | solution.py:412
  14.7 0.1 pad_add_fusion.codes_ref
  14.7 0.0 collective-permute-done.6.plus_ref
  14.7 0.0 collective-permute-done.7.minus_ref
  14.7 0.4 corner0.1
  15.2 0.6 collective-permute-start.8
  15.7 0.0 collective-permute-done.plus_ref
  15.8 0.5 collective-permute-start.10
  16.3 0.0 collective-permute-done.1.minus_ref
  16.3 0.4 corner1.1
  16.7 5.6 %collective-permute-start.3 = (f32[96,768]{1,0:T(8,128)S(1)}, f32[96,768]{1,0:T(8,128)S(1)}, u32[]{:S(2)}, u32[]{:S(2)}) collective-permute-start(f32[96,768]{1,0:T(8,128)S(1)} %get-tuple-element.30), channel_id=1, source_target_pairs={{0,31},{1,2},{2,1},{3,4},{4,3},{5,6},{6,5},{7,8},{8,7},{9,10},{10,... | collective-permute-start | bytes 884744 | tf_op jit(solution)/shard_map/ppermute | solution.py:425
  22.3 0.0 collective-permute-done.2.side_ref
  22.3 0.5 collective-permute-start.5
  22.8 1.9 %collective-permute-done.8.cross_ref = f32[96,768]{1,0:T(8,128)S(1)} collective-permute-done((f32[96,768]{1,0:T(8,128)S(1)}, f32[96,768]{1,0:T(8,128)S(1)}, u32[]{:S(2)}, u32[]{:S(2)}) %collective-permute-start.8) | collective-permute-done | bytes 294944 | tf_op jit(solution)/shard_map/ppermute | solution.py:425
  24.7 6.6 %inverse_root.1 = (f32[768,768]{1,0:T(8,128)S(1)}, bf16[768,768]{1,0:T(8,128)(2,1)S(1)}, bf16[768,768]{1,0:T(8,128)(2,1)S(1)}) custom-call(s32[1]{0:T(128)} %bitcast.odd_ref, s32[32]{0:T(128)S(1)} %pad_add_fusion.codes_ref, f32[96,896]{1,0:T(8,128)S(1)} %get-tuple-element.29.margin_ref.own_ref, f32[96,640]{1,0:T(8,128)S(1)} %collective-permute-done.6.plus_ref, ...), custom_call_target="tpu_custom_call" | custom-call | flops 3623878656 | bytes 8388608 | tf_op jit(solution)/shard_map/inverse_root/pallas_call | solution.py:433
  31.3 18.5 %density.1 = (f32[864,128]{1,0:T(8,128)S(1)}, f32[104,256]{1,0:T(8,128)S(1)}, f32[96,276]{1,0:T(8,128)S(1)}, f32[104,256]{1,0:T(8,128)S(1)}) custom-call(s32[1]{0:T(128)} %bitcast.odd_ref, s32[32]{0:T(128)S(1)} %pad_add_fusion.codes_ref, f32[1]{0:T(128)S(6)} %copy.4.chem_ref, f32[96,896]{1,0:T(8,128)S(1)} %get-tuple-element.26.ham_ref.own_ref, ...), custom_call_target="tpu_custom_call" | custom-call | flops 10871635968 | bytes 8388608 | tf_op jit(solution)/shard_map/density/pallas_call | solution.py:444
  49.8 0.3 collective-permute-start.11
  50.1 1.7 %collective-permute-start.12 = (f32[104,256]{1,0:T(8,128)S(1)}, f32[104,256]{1,0:T(8,128)S(1)}, u32[]{:S(2)}, u32[]{:S(2)}) collective-permute-start(f32[104,256]{1,0:T(8,128)S(1)} %get-tuple-element.44), channel_id=1, source_target_pairs={{32,0},{64,32},{96,64},{0,96},{33,1},{65,33},{97,65},{1,97},{34,2}... | collective-permute-start | bytes 319496 | tf_op jit(solution)/shard_map/ppermute | solution.py:457
  51.9 2.7 %collective-permute-done.11.up_ref = f32[104,256]{1,0:T(8,128)S(1)} collective-permute-done((f32[104,256]{1,0:T(8,128)S(1)}, f32[104,256]{1,0:T(8,128)S(1)}, u32[]{:S(2)}, u32[]{:S(2)}) %collective-permute-start.11) | collective-permute-done | bytes 106528 | tf_op jit(solution)/shard_map/ppermute | solution.py:456
  54.5 1.5 %collective-permute-done.12.down_ref = f32[104,256]{1,0:T(8,128)S(1)} collective-permute-done((f32[104,256]{1,0:T(8,128)S(1)}, f32[104,256]{1,0:T(8,128)S(1)}, u32[]{:S(2)}, u32[]{:S(2)}) %collective-permute-start.12) | collective-permute-done | bytes 106528 | tf_op jit(solution)/shard_map/ppermute | solution.py:457
  56.0 0.2 turn.1
  56.3 2.9 %collective-permute-start.13 = (f32[104,256]{1,0:T(8,128)S(1)}, f32[104,256]{1,0:T(8,128)S(1)}, u32[]{:S(2)}, u32[]{:S(2)}) collective-permute-start(f32[104,256]{1,0:T(8,128)S(1)} %get-tuple-element.45), channel_id=1, source_target_pairs={{0,31},{1,2},{2,1},{3,4},{4,3},{5,6},{6,5},{7,8},{8,7},{9,10},{10,... | collective-permute-start | bytes 319496 | tf_op jit(solution)/shard_map/ppermute | solution.py:475
  59.2 0.2 own.1.w_ref
  59.4 4.4 %collective-permute-done.13.cross_ref = f32[104,256]{1,0:T(8,128)S(1)} collective-permute-done((f32[104,256]{1,0:T(8,128)S(1)}, f32[104,256]{1,0:T(8,128)S(1)}, u32[]{:S(2)}, u32[]{:S(2)}) %collective-permute-start.13) | collective-permute-done | bytes 106528 | tf_op jit(solution)/shard_map/ppermute | solution.py:475
  63.8 1.0 %symmetrize.1 = f32[23,4,828]{2,1,0:T(4,128)} custom-call(s32[1]{0:T(128)} %bitcast.odd_ref, f32[7,96,128]{2,1,0:T(8,128)S(1)} %own.1.w_ref, f32[96,276]{1,0:T(8,128)S(1)} %get-tuple-element.42.mid_ref, f32[104,256]{1,0:T(8,128)S(1)} %collective-permute-done.11.up_ref, f32[104,256]{1,0:T(8,128)S(1)} %collective-permute-done.12.down_ref, ...), custom_call_target="tpu_custom_call" | custom-call | tf_op jit(solution)/shard_map/symmetrize/pallas_call | solution.py:477
  (12 shorter events, 0.0 us)
Async XLA Ops:
  0.0 14.7 %copy-start = (s32[1,1,28]{2,1,0:T(1,128)S(1)}, s32[1,1,28]{2,1,0:T(1,128)}, u32[]{:S(2)}) copy-start(s32[1,1,28]{2,1,0:T(1,128)} %param.4) | copy-start | bytes 340
  1.2 13.5 %collective-permute-start.6 = (f32[96,640]{1,0:T(8,128)S(1)}, f32[96,640]{1,0:T(8,128)S(1)}, u32[]{:S(2)}, u32[]{:S(2)}) collective-permute-start(f32[96,640]{1,0:T(8,128)S(1)} %get-tuple-element.33), channel_id=1, source_target_pairs={{32,0},{64,32},{96,64},{0,96},{33,1},{65,33},{97,65},{1,97},{34,2}... | collective-permute-start | bytes 737288 | tf_op jit(solution)/shard_map/ppermute | solution.py:401
  2.0 12.7 %collective-permute-start.7 = (f32[96,640]{1,0:T(8,128)S(1)}, f32[96,640]{1,0:T(8,128)S(1)}, u32[]{:S(2)}, u32[]{:S(2)}) collective-permute-start(f32[96,640]{1,0:T(8,128)S(1)} %get-tuple-element.34), channel_id=1, source_target_pairs={{0,32},{32,64},{64,96},{96,0},{1,33},{33,65},{65,97},{97,1},{2,34}... | collective-permute-start | bytes 737288 | tf_op jit(solution)/shard_map/ppermute | solution.py:402
  5.7 10.0 %collective-permute-start = (f32[96,640]{1,0:T(8,128)S(1)}, f32[96,640]{1,0:T(8,128)S(1)}, u32[]{:S(2)}, u32[]{:S(2)}) collective-permute-start(f32[96,640]{1,0:T(8,128)S(1)} %get-tuple-element.27), channel_id=1, source_target_pairs={{32,0},{64,32},{96,64},{0,96},{33,1},{65,33},{97,65},{1,97},{34,2}... | collective-permute-start | bytes 737288 | tf_op jit(solution)/shard_map/ppermute | solution.py:401
  5.8 10.5 %collective-permute-start.1 = (f32[96,640]{1,0:T(8,128)S(1)}, f32[96,640]{1,0:T(8,128)S(1)}, u32[]{:S(2)}, u32[]{:S(2)}) collective-permute-start(f32[96,640]{1,0:T(8,128)S(1)} %get-tuple-element.28), channel_id=1, source_target_pairs={{0,32},{32,64},{64,96},{96,0},{1,33},{33,65},{65,97},{97,1},{2,34}... | collective-permute-start | bytes 737288 | tf_op jit(solution)/shard_map/ppermute | solution.py:402
  9.4 12.9 %collective-permute-start.2 = (f32[96,1152]{1,0:T(8,128)S(1)}, f32[96,1152]{1,0:T(8,128)S(1)}, u32[]{:S(2)}, u32[]{:S(2)}) collective-permute-start(f32[96,1152]{1,0:T(8,128)S(1)} %side.1), channel_id=1, source_target_pairs={{0,31},{1,2},{2,1},{3,4},{4,3},{5,6},{6,5},{7,8},{8,7},{9,10},{10,... | collective-permute-start | bytes 1327112 | tf_op jit(solution)/shard_map/ppermute | solution.py:412
  15.2 9.5 %collective-permute-start.8 = (f32[96,768]{1,0:T(8,128)S(1)}, f32[96,768]{1,0:T(8,128)S(1)}, u32[]{:S(2)}, u32[]{:S(2)}) collective-permute-start(f32[96,768]{1,0:T(8,128)S(1)} %get-tuple-element.35), channel_id=1, source_target_pairs={{0,31},{1,2},{2,1},{3,4},{4,3},{5,6},{6,5},{7,8},{8,7},{9,10},{10,... | collective-permute-start | bytes 884744 | tf_op jit(solution)/shard_map/ppermute | solution.py:425
  15.7 9.0 %collective-permute-start.9 = (f32[96,768]{1,0:T(8,128)S(1)}, f32[96,768]{1,0:T(8,128)S(1)}, u32[]{:S(2)}, u32[]{:S(2)}) collective-permute-start(f32[96,768]{1,0:T(8,128)S(1)} %get-tuple-element.36), channel_id=1, source_target_pairs={{0,1},{1,0},{2,3},{3,2},{4,5},{5,4},{6,7},{7,6},{8,9},{9,8},{10,11... | collective-permute-start | bytes 884744 | tf_op jit(solution)/shard_map/ppermute | solution.py:425
  15.8 6.5 %collective-permute-start.10 = (f32[96,640]{1,0:T(8,128)S(1)}, f32[96,640]{1,0:T(8,128)S(1)}, u32[]{:S(2)}, u32[]{:S(2)}) collective-permute-start(f32[96,640]{1,0:T(8,128)S(1)} %get-tuple-element.37), channel_id=1, source_target_pairs={{0,1},{1,0},{2,3},{3,2},{4,5},{5,4},{6,7},{7,6},{8,9},{9,8},{10,11... | collective-permute-start | bytes 737288 | tf_op jit(solution)/shard_map/ppermute | solution.py:425
  16.7 14.6 %collective-permute-start.3 = (f32[96,768]{1,0:T(8,128)S(1)}, f32[96,768]{1,0:T(8,128)S(1)}, u32[]{:S(2)}, u32[]{:S(2)}) collective-permute-start(f32[96,768]{1,0:T(8,128)S(1)} %get-tuple-element.30), channel_id=1, source_target_pairs={{0,31},{1,2},{2,1},{3,4},{4,3},{5,6},{6,5},{7,8},{8,7},{9,10},{10,... | collective-permute-start | bytes 884744 | tf_op jit(solution)/shard_map/ppermute | solution.py:425
  22.3 9.0 %collective-permute-start.4 = (f32[96,768]{1,0:T(8,128)S(1)}, f32[96,768]{1,0:T(8,128)S(1)}, u32[]{:S(2)}, u32[]{:S(2)}) collective-permute-start(f32[96,768]{1,0:T(8,128)S(1)} %get-tuple-element.31), channel_id=1, source_target_pairs={{0,1},{1,0},{2,3},{3,2},{4,5},{5,4},{6,7},{7,6},{8,9},{9,8},{10,11... | collective-permute-start | bytes 884744 | tf_op jit(solution)/shard_map/ppermute | solution.py:425
  22.3 9.0 %collective-permute-start.5 = (f32[96,640]{1,0:T(8,128)S(1)}, f32[96,640]{1,0:T(8,128)S(1)}, u32[]{:S(2)}, u32[]{:S(2)}) collective-permute-start(f32[96,640]{1,0:T(8,128)S(1)} %get-tuple-element.32), channel_id=1, source_target_pairs={{0,1},{1,0},{2,3},{3,2},{4,5},{5,4},{6,7},{7,6},{8,9},{9,8},{10,11... | collective-permute-start | bytes 737288 | tf_op jit(solution)/shard_map/ppermute | solution.py:425
  49.8 4.8 %collective-permute-start.11 = (f32[104,256]{1,0:T(8,128)S(1)}, f32[104,256]{1,0:T(8,128)S(1)}, u32[]{:S(2)}, u32[]{:S(2)}) collective-permute-start(f32[104,256]{1,0:T(8,128)S(1)} %get-tuple-element.43), channel_id=1, source_target_pairs={{0,32},{32,64},{64,96},{96,0},{1,33},{33,65},{65,97},{97,1},{2,34}... | collective-permute-start | bytes 319496 | tf_op jit(solution)/shard_map/ppermute | solution.py:456
  50.1 5.9 %collective-permute-start.12 = (f32[104,256]{1,0:T(8,128)S(1)}, f32[104,256]{1,0:T(8,128)S(1)}, u32[]{:S(2)}, u32[]{:S(2)}) collective-permute-start(f32[104,256]{1,0:T(8,128)S(1)} %get-tuple-element.44), channel_id=1, source_target_pairs={{32,0},{64,32},{96,64},{0,96},{33,1},{65,33},{97,65},{1,97},{34,2}... | collective-permute-start | bytes 319496 | tf_op jit(solution)/shard_map/ppermute | solution.py:457
  56.3 7.5 %collective-permute-start.13 = (f32[104,256]{1,0:T(8,128)S(1)}, f32[104,256]{1,0:T(8,128)S(1)}, u32[]{:S(2)}, u32[]{:S(2)}) collective-permute-start(f32[104,256]{1,0:T(8,128)S(1)} %get-tuple-element.45), channel_id=1, source_target_pairs={{0,31},{1,2},{2,1},{3,4},{4,3},{5,6},{6,5},{7,8},{8,7},{9,10},{10,... | collective-permute-start | bytes 319496 | tf_op jit(solution)/shard_map/ppermute | solution.py:475
  59.2 4.6 %collective-permute-start.14 = (f32[104,256]{1,0:T(8,128)S(1)}, f32[104,256]{1,0:T(8,128)S(1)}, u32[]{:S(2)}, u32[]{:S(2)}) collective-permute-start(f32[104,256]{1,0:T(8,128)S(1)} %get-tuple-element.46), channel_id=1, source_target_pairs={{0,1},{1,0},{2,3},{3,2},{4,5},{5,4},{6,7},{7,6},{8,9},{9,8},{10,11... | collective-permute-start | bytes 319496 | tf_op jit(solution)/shard_map/ppermute | solution.py:476
where the time goes:
time: 65 us; the launch traced here: 64.8 us
  Pallas kernels  30 us (46%)
  starting transfers between devices  23.5 us (36%)
  waiting for transfers between devices  10.5 us (16%)
  between operations  0.79 us (1%)
    pallas_call x1, Pallas kernels, shards(): pl.pallas_call(density_kernel, out_shape=[struct((CODES * G, 128)), folde...  18.5 us
    pallas_call x1, Pallas kernels, shards(): pl.pallas_call(root_kernel, out_shape=[struct((DIM, DIM)), struct((DIM, D...  6.57 us
    ppermute x2, starting transfers between devices, shards(): lax.ppermute(x, 'gy', crossing)  6.21 us
    ppermute x2, starting transfers between devices, shards(): minus.append(lax.ppermute(up, 'gx', ahead))  5.72 us
    ppermute x1, starting transfers between devices, shards(): side = lax.ppermute(side, 'gy', crossing)  4.63 us
    ppermute x1, waiting for transfers between devices, shards(): x = lax.ppermute(x, 'gy', crossing)  4.38 us
    ppermute x1, starting transfers between devices, shards(): x = lax.ppermute(x, 'gy', crossing)  2.94 us
    ppermute x1, waiting for transfers between devices, shards(): from_minus = lax.ppermute(up, 'gx', ahead)  2.68 us
  transfers between devices with their start and end apart: 15, of which 4 were waited for; matrix products, arithmetic and copies ran while one was open for 0% of the time, Pallas kernels for 14%

commit v1 on v0

--- a/solution.py
+++ b/solution.py
@@ -202,6 +202,15 @@
             sink(i, j, block[part(i)])
 
 
+def symmetric_square(h, l, mixed, sink):
+    for j in range(3):
+        c = part(j)
+        mixed[:, c] = dot(h[...], l[:, c])
+        square = dot(h[: B * (j + 1)], h[:, c])
+        for i in range(j + 1):
+            sink(i, j, square[part(i)] + (mixed[part(i), c] + mixed[c, part(i)].T))
+
+
 def put_both(i, j, block, hi_ref, lo_ref):
     put(block, (part(i), part(j)), hi_ref, lo_ref)
     if i < j:
@@ -238,7 +247,7 @@
             value = value + jnp.where(diagonal(B, 0), 3.375, 0.0)
         put_both(i, j, value, hi2, lo2)
 
-    symmetric_product(hi, lo, hi, lo, second)
+    symmetric_square(hi, lo, picked, second)
 
     def third(i, j, block):
         value = block - (8.625 * one) * margin_ref[part(i), part(j)]
@@ -246,7 +255,7 @@
             value = value + jnp.where(diagonal(B, 0), 24.609375, 0.0)
         put_both(i, j, value * root, root_hi, root_lo)
 
-    symmetric_product(hi2, lo2, hi2, lo2, third)
+    symmetric_square(hi2, lo2, picked, third)
 
 
 def density_kernel(
@@ -287,7 +296,7 @@
             value = value + jnp.where(diagonal(B, 0), 1.5, 0.0)
         put_both(i, j, value, hi2, lo2)
 
-    symmetric_product(hi, lo, hi, lo, third)
+    symmetric_square(hi, lo, picked, third)
 
     def fourth(i, j, block):
         put_both(i, j, block * scale, hi3, lo3)
@@ -300,15 +309,21 @@
         whole = dot(both, bh[...])
         return whole[:ROWS] + whole[ROWS:] + dot(vh, bl[...])
 
-    def once(v):
-        return thin(v, hi3, lo3)
-
-    def next_sign(v):
-        return once(1.5 * v - 0.5 * once(once(v)))
+    def fifth(i, j, block):
+        put_both(i, j, block, hi2, lo2)
+
+    symmetric_square(hi3, lo3, picked, fifth)
+
+    def squared(v):
+        return thin(v, hi2, lo2)
+
+    def factor(v):
+        return 1.5 * v - 0.5 * squared(v)
 
     core = root_hi[:ROWS].astype(f32) + root_lo[:ROWS].astype(f32)
-    inside = 1.5 * core - 0.5 * next_sign(next_sign(core))
-    density = thin(core - next_sign(inside), root_hi, root_lo)
+    inside = factor(thin(core, hi3, lo3))
+    last = 1.5 * inside - 0.5 * squared(factor(factor(inside)))
+    density = thin(core - last, root_hi, root_lo)
 
     narrow[...] = jnp.zeros((128, DIM), f32)
     for m in range(MT):

time: 65 us -> 63.8 us (0.982)
  Pallas kernels: 30 us -> 28.8 us
    pallas_call x1, Pallas kernels: 18.5 us -> 17.6 us  [shards(): pl.pallas_call(density_kernel, out_shape=[struct((CODES * G, 128)), folde...]
where the time goes in v1:
time: 63.8 us; the launch traced here: 63.6 us
  Pallas kernels  28.8 us (45%)
  starting transfers between devices  23.5 us (37%)
  waiting for transfers between devices  10.5 us (16%)
  between operations  0.79 us (1%)
    pallas_call x1, Pallas kernels, shards(): pl.pallas_call(density_kernel, out_shape=[struct((CODES * G, 128)), folde...  17.6 us
    pallas_call x1, Pallas kernels, shards(): pl.pallas_call(root_kernel, out_shape=[struct((DIM, DIM)), struct((DIM, D...  6.21 us
    ppermute x2, starting transfers between devices, shards(): lax.ppermute(x, 'gy', crossing)  6.21 us
    ppermute x2, starting transfers between devices, shards(): minus.append(lax.ppermute(up, 'gx', ahead))  5.72 us
    ppermute x1, starting transfers between devices, shards(): side = lax.ppermute(side, 'gy', crossing)  4.63 us
    ppermute x1, waiting for transfers between devices, shards(): x = lax.ppermute(x, 'gy', crossing)  4.39 us
    ppermute x1, starting transfers between devices, shards(): x = lax.ppermute(x, 'gy', crossing)  2.93 us
    ppermute x1, waiting for transfers between devices, shards(): from_minus = lax.ppermute(up, 'gx', ahead)  2.68 us
  transfers between devices with their start and end apart: 15, of which 4 were waited for; matrix products, arithmetic and copies ran while one was open for 0% of the time, Pallas kernels for 14%

profile of v1, /device:TPU:24, one launch (start us, length us, event | category | flops | bytes accessed | tf_op | source)
XLA Modules:
  0.0 63.6 jit_solution(9798678435065702242)
XLA Ops:
  0.0 1.2 %pack0.1 = (f32[96,640]{1,0:T(8,128)S(1)}, f32[96,640]{1,0:T(8,128)S(1)}, f32[96,896]{1,0:T(8,128)S(1)}) custom-call(f32[2,23,4,828]{3,2,1,0:T(4,128)} %bitcast.8), custom_call_target="tpu_custom_call" | custom-call | tf_op jit(solution)/shard_map/pack0/pallas_call | solution.py:407
  1.2 0.8 %collective-permute-start.6 = (f32[96,640]{1,0:T(8,128)S(1)}, f32[96,640]{1,0:T(8,128)S(1)}, u32[]{:S(2)}, u32[]{:S(2)}) collective-permute-start(f32[96,640]{1,0:T(8,128)S(1)} %get-tuple-element.33), channel_id=1, source_target_pairs={{32,0},{64,32},{96,64},{0,96},{33,1},{65,33},{97,65},{1,97},{34,2}... | collective-permute-start | bytes 737288 | tf_op jit(solution)/shard_map/ppermute | solution.py:416
  2.0 2.5 %collective-permute-start.7 = (f32[96,640]{1,0:T(8,128)S(1)}, f32[96,640]{1,0:T(8,128)S(1)}, u32[]{:S(2)}, u32[]{:S(2)}) collective-permute-start(f32[96,640]{1,0:T(8,128)S(1)} %get-tuple-element.34), channel_id=1, source_target_pairs={{0,32},{32,64},{64,96},{96,0},{1,33},{33,65},{65,97},{97,1},{2,34}... | collective-permute-start | bytes 737288 | tf_op jit(solution)/shard_map/ppermute | solution.py:417
  4.5 1.2 %pack1.1 = (f32[96,640]{1,0:T(8,128)S(1)}, f32[96,640]{1,0:T(8,128)S(1)}, f32[96,896]{1,0:T(8,128)S(1)}) custom-call(f32[2,23,4,828]{3,2,1,0:T(4,128)} %bitcast.9), custom_call_target="tpu_custom_call" | custom-call | tf_op jit(solution)/shard_map/pack1/pallas_call | solution.py:407
  5.7 0.1 collective-permute-start
  5.8 3.2 %collective-permute-start.1 = (f32[96,640]{1,0:T(8,128)S(1)}, f32[96,640]{1,0:T(8,128)S(1)}, u32[]{:S(2)}, u32[]{:S(2)}) collective-permute-start(f32[96,640]{1,0:T(8,128)S(1)} %get-tuple-element.28), channel_id=1, source_target_pairs={{0,32},{32,64},{64,96},{96,0},{1,33},{33,65},{65,97},{97,1},{2,34}... | collective-permute-start | bytes 737288 | tf_op jit(solution)/shard_map/ppermute | solution.py:417
  9.0 0.3 side.1
  9.4 4.6 %collective-permute-start.2 = (f32[96,1152]{1,0:T(8,128)S(1)}, f32[96,1152]{1,0:T(8,128)S(1)}, u32[]{:S(2)}, u32[]{:S(2)}) collective-permute-start(f32[96,1152]{1,0:T(8,128)S(1)} %side.1), channel_id=1, source_target_pairs={{0,31},{1,2},{2,1},{3,4},{4,3},{5,6},{6,5},{7,8},{8,7},{9,10},{10,... | collective-permute-start | bytes 1327112 | tf_op jit(solution)/shard_map/ppermute | solution.py:427
  14.7 0.1 pad_add_fusion.codes_ref
  14.7 0.0 collective-permute-done.6.plus_ref
  14.7 0.0 collective-permute-done.7.minus_ref
  14.7 0.4 corner0.1
  15.2 0.6 collective-permute-start.8
  15.8 0.5 collective-permute-start.10
  16.3 0.4 corner1.1
  16.7 5.6 %collective-permute-start.3 = (f32[96,768]{1,0:T(8,128)S(1)}, f32[96,768]{1,0:T(8,128)S(1)}, u32[]{:S(2)}, u32[]{:S(2)}) collective-permute-start(f32[96,768]{1,0:T(8,128)S(1)} %get-tuple-element.30), channel_id=1, source_target_pairs={{0,31},{1,2},{2,1},{3,4},{4,3},{5,6},{6,5},{7,8},{8,7},{9,10},{10,... | collective-permute-start | bytes 884744 | tf_op jit(solution)/shard_map/ppermute | solution.py:440
  22.3 0.0 collective-permute-done.2.side_ref
  22.3 0.0 collective-permute-start.4
  22.3 0.0 collective-permute-done.10.near_ref
  22.3 0.5 collective-permute-start.5
  22.8 1.9 %collective-permute-done.8.cross_ref = f32[96,768]{1,0:T(8,128)S(1)} collective-permute-done((f32[96,768]{1,0:T(8,128)S(1)}, f32[96,768]{1,0:T(8,128)S(1)}, u32[]{:S(2)}, u32[]{:S(2)}) %collective-permute-start.8) | collective-permute-done | bytes 294944 | tf_op jit(solution)/shard_map/ppermute | solution.py:440
  24.7 6.2 %inverse_root.1 = (f32[768,768]{1,0:T(8,128)S(1)}, bf16[768,768]{1,0:T(8,128)(2,1)S(1)}, bf16[768,768]{1,0:T(8,128)(2,1)S(1)}) custom-call(s32[1]{0:T(128)} %bitcast.odd_ref, s32[32]{0:T(128)S(1)} %pad_add_fusion.codes_ref, f32[96,896]{1,0:T(8,128)S(1)} %get-tuple-element.29.margin_ref.own_ref, f32[96,640]{1,0:T(8,128)S(1)} %collective-permute-done.6.plus_ref, ...), custom_call_target="tpu_custom_call" | custom-call | flops 3623878656 | bytes 8388608 | tf_op jit(solution)/shard_map/inverse_root/pallas_call | solution.py:448
  31.0 17.6 %density.1 = (f32[864,128]{1,0:T(8,128)S(1)}, f32[104,256]{1,0:T(8,128)S(1)}, f32[96,276]{1,0:T(8,128)S(1)}, f32[104,256]{1,0:T(8,128)S(1)}) custom-call(s32[1]{0:T(128)} %bitcast.odd_ref, s32[32]{0:T(128)S(1)} %pad_add_fusion.codes_ref, f32[1]{0:T(128)S(6)} %copy.4.chem_ref, f32[96,896]{1,0:T(8,128)S(1)} %get-tuple-element.26.ham_ref.own_ref, ...), custom_call_target="tpu_custom_call" | custom-call | flops 10871635968 | bytes 8388608 | tf_op jit(solution)/shard_map/density/pallas_call | solution.py:459
  48.6 0.4 collective-permute-start.11
  49.0 1.7 %collective-permute-start.12 = (f32[104,256]{1,0:T(8,128)S(1)}, f32[104,256]{1,0:T(8,128)S(1)}, u32[]{:S(2)}, u32[]{:S(2)}) collective-permute-start(f32[104,256]{1,0:T(8,128)S(1)} %get-tuple-element.44), channel_id=1, source_target_pairs={{32,0},{64,32},{96,64},{0,96},{33,1},{65,33},{97,65},{1,97},{34,2}... | collective-permute-start | bytes 319496 | tf_op jit(solution)/shard_map/ppermute | solution.py:472
  50.7 2.7 %collective-permute-done.11.up_ref = f32[104,256]{1,0:T(8,128)S(1)} collective-permute-done((f32[104,256]{1,0:T(8,128)S(1)}, f32[104,256]{1,0:T(8,128)S(1)}, u32[]{:S(2)}, u32[]{:S(2)}) %collective-permute-start.11) | collective-permute-done | bytes 106528 | tf_op jit(solution)/shard_map/ppermute | solution.py:471
  53.4 1.5 %collective-permute-done.12.down_ref = f32[104,256]{1,0:T(8,128)S(1)} collective-permute-done((f32[104,256]{1,0:T(8,128)S(1)}, f32[104,256]{1,0:T(8,128)S(1)}, u32[]{:S(2)}, u32[]{:S(2)}) %collective-permute-start.12) | collective-permute-done | bytes 106528 | tf_op jit(solution)/shard_map/ppermute | solution.py:472
  54.9 0.2 turn.1
  55.1 2.9 %collective-permute-start.13 = (f32[104,256]{1,0:T(8,128)S(1)}, f32[104,256]{1,0:T(8,128)S(1)}, u32[]{:S(2)}, u32[]{:S(2)}) collective-permute-start(f32[104,256]{1,0:T(8,128)S(1)} %get-tuple-element.45), channel_id=1, source_target_pairs={{0,31},{1,2},{2,1},{3,4},{4,3},{5,6},{6,5},{7,8},{8,7},{9,10},{10,... | collective-permute-start | bytes 319496 | tf_op jit(solution)/shard_map/ppermute | solution.py:490
  58.0 0.2 own.1.w_ref
  58.2 4.4 %collective-permute-done.13.cross_ref = f32[104,256]{1,0:T(8,128)S(1)} collective-permute-done((f32[104,256]{1,0:T(8,128)S(1)}, f32[104,256]{1,0:T(8,128)S(1)}, u32[]{:S(2)}, u32[]{:S(2)}) %collective-permute-start.13) | collective-permute-done | bytes 106528 | tf_op jit(solution)/shard_map/ppermute | solution.py:490
  62.6 1.0 %symmetrize.1 = f32[23,4,828]{2,1,0:T(4,128)} custom-call(s32[1]{0:T(128)} %bitcast.odd_ref, f32[7,96,128]{2,1,0:T(8,128)S(1)} %own.1.w_ref, f32[96,276]{1,0:T(8,128)S(1)} %get-tuple-element.42.mid_ref, f32[104,256]{1,0:T(8,128)S(1)} %collective-permute-done.11.up_ref, f32[104,256]{1,0:T(8,128)S(1)} %collective-permute-done.12.down_ref, ...), custom_call_target="tpu_custom_call" | custom-call | tf_op jit(solution)/shard_map/symmetrize/pallas_call | solution.py:492
  (12 shorter events, 0.0 us)
Async XLA Ops:
  0.0 14.7 %copy-start = (s32[1,1,28]{2,1,0:T(1,128)S(1)}, s32[1,1,28]{2,1,0:T(1,128)}, u32[]{:S(2)}) copy-start(s32[1,1,28]{2,1,0:T(1,128)} %param.4) | copy-start | bytes 340
  1.2 13.5 %collective-permute-start.6 = (f32[96,640]{1,0:T(8,128)S(1)}, f32[96,640]{1,0:T(8,128)S(1)}, u32[]{:S(2)}, u32[]{:S(2)}) collective-permute-start(f32[96,640]{1,0:T(8,128)S(1)} %get-tuple-element.33), channel_id=1, source_target_pairs={{32,0},{64,32},{96,64},{0,96},{33,1},{65,33},{97,65},{1,97},{34,2}... | collective-permute-start | bytes 737288 | tf_op jit(solution)/shard_map/ppermute | solution.py:416
  2.0 12.7 %collective-permute-start.7 = (f32[96,640]{1,0:T(8,128)S(1)}, f32[96,640]{1,0:T(8,128)S(1)}, u32[]{:S(2)}, u32[]{:S(2)}) collective-permute-start(f32[96,640]{1,0:T(8,128)S(1)} %get-tuple-element.34), channel_id=1, source_target_pairs={{0,32},{32,64},{64,96},{96,0},{1,33},{33,65},{65,97},{97,1},{2,34}... | collective-permute-start | bytes 737288 | tf_op jit(solution)/shard_map/ppermute | solution.py:417
  5.7 10.0 %collective-permute-start = (f32[96,640]{1,0:T(8,128)S(1)}, f32[96,640]{1,0:T(8,128)S(1)}, u32[]{:S(2)}, u32[]{:S(2)}) collective-permute-start(f32[96,640]{1,0:T(8,128)S(1)} %get-tuple-element.27), channel_id=1, source_target_pairs={{32,0},{64,32},{96,64},{0,96},{33,1},{65,33},{97,65},{1,97},{34,2}... | collective-permute-start | bytes 737288 | tf_op jit(solution)/shard_map/ppermute | solution.py:416
  5.8 10.5 %collective-permute-start.1 = (f32[96,640]{1,0:T(8,128)S(1)}, f32[96,640]{1,0:T(8,128)S(1)}, u32[]{:S(2)}, u32[]{:S(2)}) collective-permute-start(f32[96,640]{1,0:T(8,128)S(1)} %get-tuple-element.28), channel_id=1, source_target_pairs={{0,32},{32,64},{64,96},{96,0},{1,33},{33,65},{65,97},{97,1},{2,34}... | collective-permute-start | bytes 737288 | tf_op jit(solution)/shard_map/ppermute | solution.py:417
  9.4 12.9 %collective-permute-start.2 = (f32[96,1152]{1,0:T(8,128)S(1)}, f32[96,1152]{1,0:T(8,128)S(1)}, u32[]{:S(2)}, u32[]{:S(2)}) collective-permute-start(f32[96,1152]{1,0:T(8,128)S(1)} %side.1), channel_id=1, source_target_pairs={{0,31},{1,2},{2,1},{3,4},{4,3},{5,6},{6,5},{7,8},{8,7},{9,10},{10,... | collective-permute-start | bytes 1327112 | tf_op jit(solution)/shard_map/ppermute | solution.py:427
  15.2 9.5 %collective-permute-start.8 = (f32[96,768]{1,0:T(8,128)S(1)}, f32[96,768]{1,0:T(8,128)S(1)}, u32[]{:S(2)}, u32[]{:S(2)}) collective-permute-start(f32[96,768]{1,0:T(8,128)S(1)} %get-tuple-element.35), channel_id=1, source_target_pairs={{0,31},{1,2},{2,1},{3,4},{4,3},{5,6},{6,5},{7,8},{8,7},{9,10},{10,... | collective-permute-start | bytes 884744 | tf_op jit(solution)/shard_map/ppermute | solution.py:440
  15.7 9.0 %collective-permute-start.9 = (f32[96,768]{1,0:T(8,128)S(1)}, f32[96,768]{1,0:T(8,128)S(1)}, u32[]{:S(2)}, u32[]{:S(2)}) collective-permute-start(f32[96,768]{1,0:T(8,128)S(1)} %get-tuple-element.36), channel_id=1, source_target_pairs={{0,1},{1,0},{2,3},{3,2},{4,5},{5,4},{6,7},{7,6},{8,9},{9,8},{10,11... | collective-permute-start | bytes 884744 | tf_op jit(solution)/shard_map/ppermute | solution.py:440
  15.8 6.5 %collective-permute-start.10 = (f32[96,640]{1,0:T(8,128)S(1)}, f32[96,640]{1,0:T(8,128)S(1)}, u32[]{:S(2)}, u32[]{:S(2)}) collective-permute-start(f32[96,640]{1,0:T(8,128)S(1)} %get-tuple-element.37), channel_id=1, source_target_pairs={{0,1},{1,0},{2,3},{3,2},{4,5},{5,4},{6,7},{7,6},{8,9},{9,8},{10,11... | collective-permute-start | bytes 737288 | tf_op jit(solution)/shard_map/ppermute | solution.py:440
  16.7 14.3 %collective-permute-start.3 = (f32[96,768]{1,0:T(8,128)S(1)}, f32[96,768]{1,0:T(8,128)S(1)}, u32[]{:S(2)}, u32[]{:S(2)}) collective-permute-start(f32[96,768]{1,0:T(8,128)S(1)} %get-tuple-element.30), channel_id=1, source_target_pairs={{0,31},{1,2},{2,1},{3,4},{4,3},{5,6},{6,5},{7,8},{8,7},{9,10},{10,... | collective-permute-start | bytes 884744 | tf_op jit(solution)/shard_map/ppermute | solution.py:440
  22.3 8.7 %collective-permute-start.4 = (f32[96,768]{1,0:T(8,128)S(1)}, f32[96,768]{1,0:T(8,128)S(1)}, u32[]{:S(2)}, u32[]{:S(2)}) collective-permute-start(f32[96,768]{1,0:T(8,128)S(1)} %get-tuple-element.31), channel_id=1, source_target_pairs={{0,1},{1,0},{2,3},{3,2},{4,5},{5,4},{6,7},{7,6},{8,9},{9,8},{10,11... | collective-permute-start | bytes 884744 | tf_op jit(solution)/shard_map/ppermute | solution.py:440
  22.3 8.6 %collective-permute-start.5 = (f32[96,640]{1,0:T(8,128)S(1)}, f32[96,640]{1,0:T(8,128)S(1)}, u32[]{:S(2)}, u32[]{:S(2)}) collective-permute-start(f32[96,640]{1,0:T(8,128)S(1)} %get-tuple-element.32), channel_id=1, source_target_pairs={{0,1},{1,0},{2,3},{3,2},{4,5},{5,4},{6,7},{7,6},{8,9},{9,8},{10,11... | collective-permute-start | bytes 737288 | tf_op jit(solution)/shard_map/ppermute | solution.py:440
  48.6 4.8 %collective-permute-start.11 = (f32[104,256]{1,0:T(8,128)S(1)}, f32[104,256]{1,0:T(8,128)S(1)}, u32[]{:S(2)}, u32[]{:S(2)}) collective-permute-start(f32[104,256]{1,0:T(8,128)S(1)} %get-tuple-element.43), channel_id=1, source_target_pairs={{0,32},{32,64},{64,96},{96,0},{1,33},{33,65},{65,97},{97,1},{2,34}... | collective-permute-start | bytes 319496 | tf_op jit(solution)/shard_map/ppermute | solution.py:471
  49.0 5.9 %collective-permute-start.12 = (f32[104,256]{1,0:T(8,128)S(1)}, f32[104,256]{1,0:T(8,128)S(1)}, u32[]{:S(2)}, u32[]{:S(2)}) collective-permute-start(f32[104,256]{1,0:T(8,128)S(1)} %get-tuple-element.44), channel_id=1, source_target_pairs={{32,0},{64,32},{96,64},{0,96},{33,1},{65,33},{97,65},{1,97},{34,2}... | collective-permute-start | bytes 319496 | tf_op jit(solution)/shard_map/ppermute | solution.py:472
  55.1 7.5 %collective-permute-start.13 = (f32[104,256]{1,0:T(8,128)S(1)}, f32[104,256]{1,0:T(8,128)S(1)}, u32[]{:S(2)}, u32[]{:S(2)}) collective-permute-start(f32[104,256]{1,0:T(8,128)S(1)} %get-tuple-element.45), channel_id=1, source_target_pairs={{0,31},{1,2},{2,1},{3,4},{4,3},{5,6},{6,5},{7,8},{8,7},{9,10},{10,... | collective-permute-start | bytes 319496 | tf_op jit(solution)/shard_map/ppermute | solution.py:490
  58.0 4.6 %collective-permute-start.14 = (f32[104,256]{1,0:T(8,128)S(1)}, f32[104,256]{1,0:T(8,128)S(1)}, u32[]{:S(2)}, u32[]{:S(2)}) collective-permute-start(f32[104,256]{1,0:T(8,128)S(1)} %get-tuple-element.46), channel_id=1, source_target_pairs={{0,1},{1,0},{2,3},{3,2},{4,5},{5,4},{6,7},{7,6},{8,9},{9,8},{10,11... | collective-permute-start | bytes 319496 | tf_op jit(solution)/shard_map/ppermute | solution.py:491

commit v2 on v1

--- a/solution.py
+++ b/solution.py
@@ -63,22 +63,22 @@
     return jnp.concatenate([ref[:ROWS], last], axis=1)
 
 
-def pack_kernel(q, blocks_ref, down_ref, up_ref, own_ref, held, sems):
-    cuts = (0, 6, 12, 18, F)
-    copies = []
-    for n in range(4):
-        f = pl.ds(cuts[n], cuts[n + 1] - cuts[n])
-        copies.append(pltpu.make_async_copy(blocks_ref.at[q, f], held.at[f], sems.at[n]))
-    for copy in copies:
-        copy.start()
-    for copy in copies:
-        copy.wait()
-    parts = [held[f] for f in range(F)] + [jnp.zeros((MT, WIDE), f32)]
-    own = jnp.concatenate(parts, axis=0)
+def pack(held, down_ref, up_ref, own_ref):
+    own = jnp.concatenate([held[f] for f in range(F)] + [jnp.zeros((MT, WIDE), f32)], axis=0)
     own_ref[:, :WIDE] = own
     own_ref[:, WIDE:] = jnp.zeros((ROWS, LANES - WIDE), f32)
     down_ref[...] = own[:, :EDGE]
     up_ref[...] = jnp.concatenate([own[:, 276:], blank(EDGE - 552)], axis=1)
+
+
+def margin_pack_kernel(blocks_ref, down_ref, up_ref, own_ref, ham_ref, held, sems):
+    first = pltpu.make_async_copy(blocks_ref.at[0], held, sems.at[0])
+    second = pltpu.make_async_copy(blocks_ref.at[1], ham_ref, sems.at[1])
+    first.start()
+    second.start()
+    first.wait()
+    pack(held, down_ref, up_ref, own_ref)
+    second.wait()
 
 
 def blank(width):
@@ -403,16 +403,27 @@
     native = pltpu.with_memory_space_constraint(jnp.transpose(blocks[0, 0], (0, 2, 1, 3)), pltpu.HBM)
 
     plus, minus, own = [], [], []
+    packed = [struct((ROWS, EDGE)), struct((ROWS, EDGE)), struct((ROWS, LANES))]
+    down, up, mine, ham = pl.pallas_call(
+        margin_pack_kernel,
+        out_shape=packed + [struct((F, MT, WIDE))],
+        in_specs=[ANY],
+        out_specs=[VMEM] * 4,
+        scratch_shapes=[pltpu.VMEM((F, MT, WIDE), f32), pltpu.SemaphoreType.DMA((2,))],
+        name="pack0",
+        compiler_params=params(),
+    )(native)
     for q in range(2):
-        down, up, mine = pl.pallas_call(
-            functools.partial(pack_kernel, q),
-            out_shape=[struct((ROWS, EDGE)), struct((ROWS, EDGE)), struct((ROWS, LANES))],
-            in_specs=[ANY],
-            out_specs=[VMEM] * 3,
-            scratch_shapes=[pltpu.VMEM((F, MT, WIDE), f32), pltpu.SemaphoreType.DMA((4,))],
-            name=f"pack{q}",
-            compiler_params=params(),
-        )(native)
+        if q:
+            down, up, mine = pl.pallas_call(
+                pack,
+                out_shape=packed,
+                in_specs=[VMEM],
+                out_specs=[VMEM] * 3,
+                name="pack1",
+                compiler_params=params(),
+                cost_estimate=pl.CostEstimate(flops=10**6, bytes_accessed=10**6, transcendentals=0),
+            )(ham)
         plus.append(lax.ppermute(down, "gx", back))
         minus.append(lax.ppermute(up, "gx", ahead))
         own.append(mine)

time: 63.8 us -> 63.3 us (level)
  Pallas kernels: 28.8 us -> 27.7 us
    pallas_call x2, Pallas kernels: 2.38 us -> 1.28 us  [the longest x1 1.15 us: shards(): pl.pallas_call(margin_pack_kernel, out_shape=packed + [struct((F, MT, WID...]
    ppermute x2, waiting for transfers between devices: 1.9 us -> 0.85 us  [shards(): lax.ppermute(x, 'gy', crossing)]
    ppermute x2, starting transfers between devices: 6.21 us -> 7.26 us  [shards(): lax.ppermute(x, 'gy', crossing)]
  transfers between devices with their start and end apart: 15 -> 15, of which waited for: 4 -> 4; matrix products, arithmetic and copies ran while one was open for 0% -> 0% of each run, Pallas kernels for 14% -> 12%
where the time goes in v2:
time: 63.3 us; the launch traced here: 63.2 us
  Pallas kernels  27.7 us (44%)
  starting transfers between devices  23.9 us (38%)
  waiting for transfers between devices  10.7 us (17%)
  between operations  0.79 us (1%)
    pallas_call x1, Pallas kernels, shards(): pl.pallas_call(density_kernel, out_shape=[struct((CODES * G, 128)), folde...  17.6 us
    ppermute x2, starting transfers between devices, shards(): lax.ppermute(x, 'gy', crossing)  7.26 us
    pallas_call x1, Pallas kernels, shards(): pl.pallas_call(root_kernel, out_shape=[struct((DIM, DIM)), struct((DIM, D...  6.21 us
    ppermute x2, starting transfers between devices, shards(): minus.append(lax.ppermute(up, 'gx', ahead))  5.72 us
    ppermute x1, waiting for transfers between devices, shards(): x = lax.ppermute(x, 'gy', crossing)  5.02 us
    ppermute x1, starting transfers between devices, shards(): side = lax.ppermute(side, 'gy', crossing)  4.63 us
    ppermute x1, waiting for transfers between devices, shards(): from_minus = lax.ppermute(up, 'gx', ahead)  2.68 us
    ppermute x1, starting transfers between devices, shards(): x = lax.ppermute(x, 'gy', crossing)  2.3 us
  transfers between devices with their start and end apart: 15, of which 4 were waited for; matrix products, arithmetic and copies ran while one was open for 0% of the time, Pallas kernels for 12%

profile of v2, /device:TPU:24, one launch (start us, length us, event | category | flops | bytes accessed | tf_op | source)
XLA Modules:
  0.0 63.2 jit_solution(5498461622398899294)
XLA Ops:
  0.0 1.1 %pack0.1 = (f32[96,640]{1,0:T(8,128)S(1)}, f32[96,640]{1,0:T(8,128)S(1)}, f32[96,896]{1,0:T(8,128)S(1)}, f32[23,4,828]{2,1,0:T(4,128)S(1)}) custom-call(f32[2,23,4,828]{3,2,1,0:T(4,128)} %bitcast.8), custom_call_target="tpu_custom_call" | custom-call | tf_op jit(solution)/shard_map/pack0/pallas_call | solution.py:407
  1.2 0.8 %collective-permute-start.6 = (f32[96,640]{1,0:T(8,128)S(1)}, f32[96,640]{1,0:T(8,128)S(1)}, u32[]{:S(2)}, u32[]{:S(2)}) collective-permute-start(f32[96,640]{1,0:T(8,128)S(1)} %get-tuple-element.35), channel_id=1, source_target_pairs={{32,0},{64,32},{96,64},{0,96},{33,1},{65,33},{97,65},{1,97},{34,2}... | collective-permute-start | bytes 737288 | tf_op jit(solution)/shard_map/ppermute | solution.py:427
  2.0 2.5 %collective-permute-start.7 = (f32[96,640]{1,0:T(8,128)S(1)}, f32[96,640]{1,0:T(8,128)S(1)}, u32[]{:S(2)}, u32[]{:S(2)}) collective-permute-start(f32[96,640]{1,0:T(8,128)S(1)} %get-tuple-element.36), channel_id=1, source_target_pairs={{0,32},{32,64},{64,96},{96,0},{1,33},{33,65},{65,97},{97,1},{2,34}... | collective-permute-start | bytes 737288 | tf_op jit(solution)/shard_map/ppermute | solution.py:428
  4.5 0.1 pack1.1
  4.6 0.1 collective-permute-start
  4.7 3.2 %collective-permute-start.1 = (f32[96,640]{1,0:T(8,128)S(1)}, f32[96,640]{1,0:T(8,128)S(1)}, u32[]{:S(2)}, u32[]{:S(2)}) collective-permute-start(f32[96,640]{1,0:T(8,128)S(1)} %get-tuple-element.30), channel_id=1, source_target_pairs={{0,32},{32,64},{64,96},{96,0},{1,33},{33,65},{65,97},{97,1},{2,34}... | collective-permute-start | bytes 737288 | tf_op jit(solution)/shard_map/ppermute | solution.py:428
  7.9 0.3 side.1
  8.3 4.6 %collective-permute-start.2 = (f32[96,1152]{1,0:T(8,128)S(1)}, f32[96,1152]{1,0:T(8,128)S(1)}, u32[]{:S(2)}, u32[]{:S(2)}) collective-permute-start(f32[96,1152]{1,0:T(8,128)S(1)} %side.1), channel_id=1, source_target_pairs={{0,31},{1,2},{2,1},{3,4},{4,3},{5,6},{6,5},{7,8},{8,7},{9,10},{10,... | collective-permute-start | bytes 1327112 | tf_op jit(solution)/shard_map/ppermute | solution.py:438
  13.6 0.1 pad_add_fusion.codes_ref
  13.6 0.0 collective-permute-done.7.minus_ref
  13.6 0.4 corner0.1
  14.1 1.4 %collective-permute-start.8 = (f32[96,768]{1,0:T(8,128)S(1)}, f32[96,768]{1,0:T(8,128)S(1)}, u32[]{:S(2)}, u32[]{:S(2)}) collective-permute-start(f32[96,768]{1,0:T(8,128)S(1)} %get-tuple-element.37), channel_id=1, source_target_pairs={{0,31},{1,2},{2,1},{3,4},{4,3},{5,6},{6,5},{7,8},{8,7},{9,10},{10,... | collective-permute-start | bytes 884744 | tf_op jit(solution)/shard_map/ppermute | solution.py:451
  15.4 0.0 collective-permute-done.plus_ref
  15.4 0.5 collective-permute-start.10
  15.9 0.0 collective-permute-done.1.minus_ref
  15.9 0.4 corner1.1
  16.3 5.9 %collective-permute-start.3 = (f32[96,768]{1,0:T(8,128)S(1)}, f32[96,768]{1,0:T(8,128)S(1)}, u32[]{:S(2)}, u32[]{:S(2)}) collective-permute-start(f32[96,768]{1,0:T(8,128)S(1)} %get-tuple-element.32), channel_id=1, source_target_pairs={{0,31},{1,2},{2,1},{3,4},{4,3},{5,6},{6,5},{7,8},{8,7},{9,10},{10,... | collective-permute-start | bytes 884744 | tf_op jit(solution)/shard_map/ppermute | solution.py:451
  22.2 0.5 collective-permute-start.5
  22.8 0.8 %collective-permute-done.8.cross_ref = f32[96,768]{1,0:T(8,128)S(1)} collective-permute-done((f32[96,768]{1,0:T(8,128)S(1)}, f32[96,768]{1,0:T(8,128)S(1)}, u32[]{:S(2)}, u32[]{:S(2)}) %collective-permute-start.8) | collective-permute-done | bytes 294944 | tf_op jit(solution)/shard_map/ppermute | solution.py:451
  23.6 6.2 %inverse_root.1 = (f32[768,768]{1,0:T(8,128)S(1)}, bf16[768,768]{1,0:T(8,128)(2,1)S(1)}, bf16[768,768]{1,0:T(8,128)(2,1)S(1)}) custom-call(s32[1]{0:T(128)} %bitcast.odd_ref, s32[32]{0:T(128)S(1)} %pad_add_fusion.codes_ref, f32[96,896]{1,0:T(8,128)S(1)} %get-tuple-element.31.margin_ref.own_ref, f32[96,640]{1,0:T(8,128)S(1)} %collective-permute-done.6.plus_ref, ...), custom_call_target="tpu_custom_call" | custom-call | flops 3623878656 | bytes 8388608 | tf_op jit(solution)/shard_map/inverse_root/pallas_call | solution.py:459
  29.8 0.0 collective-permute-done.5.near_ref
  29.8 0.0 collective-permute-done.3.cross_ref
  29.9 17.6 %density.1 = (f32[864,128]{1,0:T(8,128)S(1)}, f32[104,256]{1,0:T(8,128)S(1)}, f32[96,276]{1,0:T(8,128)S(1)}, f32[104,256]{1,0:T(8,128)S(1)}) custom-call(s32[1]{0:T(128)} %bitcast.odd_ref, s32[32]{0:T(128)S(1)} %pad_add_fusion.codes_ref, f32[1]{0:T(128)S(6)} %copy.4.chem_ref, f32[96,896]{1,0:T(8,128)S(1)} %get-tuple-element.28.ham_ref.own_ref, ...), custom_call_target="tpu_custom_call" | custom-call | flops 10871635968 | bytes 8388608 | tf_op jit(solution)/shard_map/density/pallas_call | solution.py:470
  47.5 1.0 %collective-permute-start.11 = (f32[104,256]{1,0:T(8,128)S(1)}, f32[104,256]{1,0:T(8,128)S(1)}, u32[]{:S(2)}, u32[]{:S(2)}) collective-permute-start(f32[104,256]{1,0:T(8,128)S(1)} %get-tuple-element.45), channel_id=1, source_target_pairs={{0,32},{32,64},{64,96},{96,0},{1,33},{33,65},{65,97},{97,1},{2,34}... | collective-permute-start | bytes 319496 | tf_op jit(solution)/shard_map/ppermute | solution.py:482
  48.5 1.1 %collective-permute-start.12 = (f32[104,256]{1,0:T(8,128)S(1)}, f32[104,256]{1,0:T(8,128)S(1)}, u32[]{:S(2)}, u32[]{:S(2)}) collective-permute-start(f32[104,256]{1,0:T(8,128)S(1)} %get-tuple-element.46), channel_id=1, source_target_pairs={{32,0},{64,32},{96,64},{0,96},{33,1},{65,33},{97,65},{1,97},{34,2}... | collective-permute-start | bytes 319496 | tf_op jit(solution)/shard_map/ppermute | solution.py:483
  49.6 2.7 %collective-permute-done.11.up_ref = f32[104,256]{1,0:T(8,128)S(1)} collective-permute-done((f32[104,256]{1,0:T(8,128)S(1)}, f32[104,256]{1,0:T(8,128)S(1)}, u32[]{:S(2)}, u32[]{:S(2)}) %collective-permute-start.11) | collective-permute-done | bytes 106528 | tf_op jit(solution)/shard_map/ppermute | solution.py:482
  52.3 2.1 %collective-permute-done.12.down_ref = f32[104,256]{1,0:T(8,128)S(1)} collective-permute-done((f32[104,256]{1,0:T(8,128)S(1)}, f32[104,256]{1,0:T(8,128)S(1)}, u32[]{:S(2)}, u32[]{:S(2)}) %collective-permute-start.12) | collective-permute-done | bytes 106528 | tf_op jit(solution)/shard_map/ppermute | solution.py:483
  54.4 0.2 turn.1
  54.6 2.3 %collective-permute-start.13 = (f32[104,256]{1,0:T(8,128)S(1)}, f32[104,256]{1,0:T(8,128)S(1)}, u32[]{:S(2)}, u32[]{:S(2)}) collective-permute-start(f32[104,256]{1,0:T(8,128)S(1)} %get-tuple-element.47), channel_id=1, source_target_pairs={{0,31},{1,2},{2,1},{3,4},{4,3},{5,6},{6,5},{7,8},{8,7},{9,10},{10,... | collective-permute-start | bytes 319496 | tf_op jit(solution)/shard_map/ppermute | solution.py:501
  56.9 0.2 own.1.w_ref
  57.1 5.0 %collective-permute-done.13.cross_ref = f32[104,256]{1,0:T(8,128)S(1)} collective-permute-done((f32[104,256]{1,0:T(8,128)S(1)}, f32[104,256]{1,0:T(8,128)S(1)}, u32[]{:S(2)}, u32[]{:S(2)}) %collective-permute-start.13) | collective-permute-done | bytes 106528 | tf_op jit(solution)/shard_map/ppermute | solution.py:501
  62.2 1.0 %symmetrize.1 = f32[23,4,828]{2,1,0:T(4,128)} custom-call(s32[1]{0:T(128)} %bitcast.odd_ref, f32[7,96,128]{2,1,0:T(8,128)S(1)} %own.1.w_ref, f32[96,276]{1,0:T(8,128)S(1)} %get-tuple-element.44.mid_ref, f32[104,256]{1,0:T(8,128)S(1)} %collective-permute-done.11.up_ref, f32[104,256]{1,0:T(8,128)S(1)} %collective-permute-done.12.down_ref, ...), custom_call_target="tpu_custom_call" | custom-call | tf_op jit(solution)/shard_map/symmetrize/pallas_call | solution.py:503
  (12 shorter events, 0.0 us)
Async XLA Ops:
  0.0 13.6 %copy-start = (s32[1,1,28]{2,1,0:T(1,128)S(1)}, s32[1,1,28]{2,1,0:T(1,128)}, u32[]{:S(2)}) copy-start(s32[1,1,28]{2,1,0:T(1,128)} %param.4) | copy-start | bytes 340
  1.2 12.5 %collective-permute-start.6 = (f32[96,640]{1,0:T(8,128)S(1)}, f32[96,640]{1,0:T(8,128)S(1)}, u32[]{:S(2)}, u32[]{:S(2)}) collective-permute-start(f32[96,640]{1,0:T(8,128)S(1)} %get-tuple-element.35), channel_id=1, source_target_pairs={{32,0},{64,32},{96,64},{0,96},{33,1},{65,33},{97,65},{1,97},{34,2}... | collective-permute-start | bytes 737288 | tf_op jit(solution)/shard_map/ppermute | solution.py:427
  2.0 11.7 %collective-permute-start.7 = (f32[96,640]{1,0:T(8,128)S(1)}, f32[96,640]{1,0:T(8,128)S(1)}, u32[]{:S(2)}, u32[]{:S(2)}) collective-permute-start(f32[96,640]{1,0:T(8,128)S(1)} %get-tuple-element.36), channel_id=1, source_target_pairs={{0,32},{32,64},{64,96},{96,0},{1,33},{33,65},{65,97},{97,1},{2,34}... | collective-permute-start | bytes 737288 | tf_op jit(solution)/shard_map/ppermute | solution.py:428
  4.6 10.8 %collective-permute-start = (f32[96,640]{1,0:T(8,128)S(1)}, f32[96,640]{1,0:T(8,128)S(1)}, u32[]{:S(2)}, u32[]{:S(2)}) collective-permute-start(f32[96,640]{1,0:T(8,128)S(1)} %get-tuple-element.29), channel_id=1, source_target_pairs={{32,0},{64,32},{96,64},{0,96},{33,1},{65,33},{97,65},{1,97},{34,2}... | collective-permute-start | bytes 737288 | tf_op jit(solution)/shard_map/ppermute | solution.py:427
  4.7 11.2 %collective-permute-start.1 = (f32[96,640]{1,0:T(8,128)S(1)}, f32[96,640]{1,0:T(8,128)S(1)}, u32[]{:S(2)}, u32[]{:S(2)}) collective-permute-start(f32[96,640]{1,0:T(8,128)S(1)} %get-tuple-element.30), channel_id=1, source_target_pairs={{0,32},{32,64},{64,96},{96,0},{1,33},{33,65},{65,97},{97,1},{2,34}... | collective-permute-start | bytes 737288 | tf_op jit(solution)/shard_map/ppermute | solution.py:428
  8.3 14.0 %collective-permute-start.2 = (f32[96,1152]{1,0:T(8,128)S(1)}, f32[96,1152]{1,0:T(8,128)S(1)}, u32[]{:S(2)}, u32[]{:S(2)}) collective-permute-start(f32[96,1152]{1,0:T(8,128)S(1)} %side.1), channel_id=1, source_target_pairs={{0,31},{1,2},{2,1},{3,4},{4,3},{5,6},{6,5},{7,8},{8,7},{9,10},{10,... | collective-permute-start | bytes 1327112 | tf_op jit(solution)/shard_map/ppermute | solution.py:438
  14.1 9.5 %collective-permute-start.8 = (f32[96,768]{1,0:T(8,128)S(1)}, f32[96,768]{1,0:T(8,128)S(1)}, u32[]{:S(2)}, u32[]{:S(2)}) collective-permute-start(f32[96,768]{1,0:T(8,128)S(1)} %get-tuple-element.37), channel_id=1, source_target_pairs={{0,31},{1,2},{2,1},{3,4},{4,3},{5,6},{6,5},{7,8},{8,7},{9,10},{10,... | collective-permute-start | bytes 884744 | tf_op jit(solution)/shard_map/ppermute | solution.py:451
  15.4 8.2 %collective-permute-start.9 = (f32[96,768]{1,0:T(8,128)S(1)}, f32[96,768]{1,0:T(8,128)S(1)}, u32[]{:S(2)}, u32[]{:S(2)}) collective-permute-start(f32[96,768]{1,0:T(8,128)S(1)} %get-tuple-element.38), channel_id=1, source_target_pairs={{0,1},{1,0},{2,3},{3,2},{4,5},{5,4},{6,7},{7,6},{8,9},{9,8},{10,11... | collective-permute-start | bytes 884744 | tf_op jit(solution)/shard_map/ppermute | solution.py:451
  15.4 6.8 %collective-permute-start.10 = (f32[96,640]{1,0:T(8,128)S(1)}, f32[96,640]{1,0:T(8,128)S(1)}, u32[]{:S(2)}, u32[]{:S(2)}) collective-permute-start(f32[96,640]{1,0:T(8,128)S(1)} %get-tuple-element.39), channel_id=1, source_target_pairs={{0,1},{1,0},{2,3},{3,2},{4,5},{5,4},{6,7},{7,6},{8,9},{9,8},{10,11... | collective-permute-start | bytes 737288 | tf_op jit(solution)/shard_map/ppermute | solution.py:451
  16.3 13.5 %collective-permute-start.3 = (f32[96,768]{1,0:T(8,128)S(1)}, f32[96,768]{1,0:T(8,128)S(1)}, u32[]{:S(2)}, u32[]{:S(2)}) collective-permute-start(f32[96,768]{1,0:T(8,128)S(1)} %get-tuple-element.32), channel_id=1, source_target_pairs={{0,31},{1,2},{2,1},{3,4},{4,3},{5,6},{6,5},{7,8},{8,7},{9,10},{10,... | collective-permute-start | bytes 884744 | tf_op jit(solution)/shard_map/ppermute | solution.py:451
  22.2 7.6 %collective-permute-start.4 = (f32[96,768]{1,0:T(8,128)S(1)}, f32[96,768]{1,0:T(8,128)S(1)}, u32[]{:S(2)}, u32[]{:S(2)}) collective-permute-start(f32[96,768]{1,0:T(8,128)S(1)} %get-tuple-element.33), channel_id=1, source_target_pairs={{0,1},{1,0},{2,3},{3,2},{4,5},{5,4},{6,7},{7,6},{8,9},{9,8},{10,11... | collective-permute-start | bytes 884744 | tf_op jit(solution)/shard_map/ppermute | solution.py:451
  22.2 7.6 %collective-permute-start.5 = (f32[96,640]{1,0:T(8,128)S(1)}, f32[96,640]{1,0:T(8,128)S(1)}, u32[]{:S(2)}, u32[]{:S(2)}) collective-permute-start(f32[96,640]{1,0:T(8,128)S(1)} %get-tuple-element.34), channel_id=1, source_target_pairs={{0,1},{1,0},{2,3},{3,2},{4,5},{5,4},{6,7},{7,6},{8,9},{9,8},{10,11... | collective-permute-start | bytes 737288 | tf_op jit(solution)/shard_map/ppermute | solution.py:451
  47.5 4.8 %collective-permute-start.11 = (f32[104,256]{1,0:T(8,128)S(1)}, f32[104,256]{1,0:T(8,128)S(1)}, u32[]{:S(2)}, u32[]{:S(2)}) collective-permute-start(f32[104,256]{1,0:T(8,128)S(1)} %get-tuple-element.45), channel_id=1, source_target_pairs={{0,32},{32,64},{64,96},{96,0},{1,33},{33,65},{65,97},{97,1},{2,34}... | collective-permute-start | bytes 319496 | tf_op jit(solution)/shard_map/ppermute | solution.py:482
  48.5 5.9 %collective-permute-start.12 = (f32[104,256]{1,0:T(8,128)S(1)}, f32[104,256]{1,0:T(8,128)S(1)}, u32[]{:S(2)}, u32[]{:S(2)}) collective-permute-start(f32[104,256]{1,0:T(8,128)S(1)} %get-tuple-element.46), channel_id=1, source_target_pairs={{32,0},{64,32},{96,64},{0,96},{33,1},{65,33},{97,65},{1,97},{34,2}... | collective-permute-start | bytes 319496 | tf_op jit(solution)/shard_map/ppermute | solution.py:483
  54.6 7.5 %collective-permute-start.13 = (f32[104,256]{1,0:T(8,128)S(1)}, f32[104,256]{1,0:T(8,128)S(1)}, u32[]{:S(2)}, u32[]{:S(2)}) collective-permute-start(f32[104,256]{1,0:T(8,128)S(1)} %get-tuple-element.47), channel_id=1, source_target_pairs={{0,31},{1,2},{2,1},{3,4},{4,3},{5,6},{6,5},{7,8},{8,7},{9,10},{10,... | collective-permute-start | bytes 319496 | tf_op jit(solution)/shard_map/ppermute | solution.py:501
  56.9 5.2 %collective-permute-start.14 = (f32[104,256]{1,0:T(8,128)S(1)}, f32[104,256]{1,0:T(8,128)S(1)}, u32[]{:S(2)}, u32[]{:S(2)}) collective-permute-start(f32[104,256]{1,0:T(8,128)S(1)} %get-tuple-element.48), channel_id=1, source_target_pairs={{0,1},{1,0},{2,3},{3,2},{4,5},{5,4},{6,7},{7,6},{8,9},{9,8},{10,11... | collective-permute-start | bytes 319496 | tf_op jit(solution)/shard_map/ppermute | solution.py:502

commit v3 on v2

--- a/solution.py
+++ b/solution.py
@@ -63,12 +63,20 @@
     return jnp.concatenate([ref[:ROWS], last], axis=1)
 
 
+def edge(ref):
+    return unfold(ref, 40) if ref.shape[1] < EDGE else ref[:, :552]
+
+
 def pack(held, down_ref, up_ref, own_ref):
     own = jnp.concatenate([held[f] for f in range(F)] + [jnp.zeros((MT, WIDE), f32)], axis=0)
     own_ref[:, :WIDE] = own
     own_ref[:, WIDE:] = jnp.zeros((ROWS, LANES - WIDE), f32)
-    down_ref[...] = own[:, :EDGE]
-    up_ref[...] = jnp.concatenate([own[:, 276:], blank(EDGE - 552)], axis=1)
+    if down_ref.shape[1] < EDGE:
+        fold(own[:, :552], down_ref)
+        fold(own[:, 276:], up_ref)
+    else:
+        down_ref[...] = own[:, :EDGE]
+        up_ref[...] = jnp.concatenate([own[:, 276:], blank(EDGE - 552)], axis=1)
 
 
 def margin_pack_kernel(blocks_ref, down_ref, up_ref, own_ref, ham_ref, held, sems):
@@ -94,7 +102,7 @@
 
 
 def corner_kernel(odd_ref, own_ref, plus_ref, minus_ref, cross_ref, inner_ref, near_ref):
-    rows = (plus_ref[:, :552], minus_ref[:, :552])
+    rows = (edge(plus_ref), edge(minus_ref))
     own = own_ref[...]
 
     def packed(o):
@@ -143,8 +151,8 @@
             rows[c, t * ROWS : (t + 1) * ROWS] = v[:, 128 * c : 128 * (c + 1)]
 
     set_rows(4, own_ref[...])
-    set_rows(7, jnp.concatenate([blank(276), plus_ref[:, :552], blank(LANES - 828)], axis=1))
-    set_rows(1, jnp.concatenate([minus_ref[:, :552], blank(LANES - 552)], axis=1))
+    set_rows(7, jnp.concatenate([blank(276), edge(plus_ref), blank(LANES - 828)], axis=1))
+    set_rows(1, jnp.concatenate([edge(minus_ref), blank(LANES - 552)], axis=1))
     set_rows(9, blank(LANES))
 
     def place(side_ref, begin, corner_ref, ahead):
@@ -406,7 +414,7 @@
     packed = [struct((ROWS, EDGE)), struct((ROWS, EDGE)), struct((ROWS, LANES))]
     down, up, mine, ham = pl.pallas_call(
         margin_pack_kernel,
-        out_shape=packed + [struct((F, MT, WIDE))],
+        out_shape=[struct((ROWS + 8, 512)), struct((ROWS + 8, 512)), packed[2], struct((F, MT, WIDE))],
         in_specs=[ANY],
         out_specs=[VMEM] * 4,
         scratch_shapes=[pltpu.VMEM((F, MT, WIDE), f32), pltpu.SemaphoreType.DMA((2,))],

time: 63.3 us -> 66.6 us (1.052)
  waiting for transfers between devices: 10.7 us -> 12.9 us
  starting transfers between devices: 23.9 us -> 25 us
    ppermute x1, starting transfers between devices: 0.98 us -> 3.02 us  [shards(): from_minus = lax.ppermute(up, 'gx', ahead)]
    ppermute x1, waiting for transfers between devices: 2.12 us -> 3.62 us  [shards(): from_plus = lax.ppermute(down, 'gx', back)]
    ppermute x1, starting transfers between devices: 2.3 us -> 3.58 us  [shards(): x = lax.ppermute(x, 'gy', crossing)]
    ppermute x1, waiting for transfers between devices: 5.02 us -> 3.74 us  [shards(): x = lax.ppermute(x, 'gy', crossing)]
    ppermute x2, waiting for transfers between devices: 0.01 us -> 1.27 us  [shards(): plus.append(lax.ppermute(down, 'gx', back))]
    ppermute x1, starting transfers between devices: 1.12 us -> 0.01 us  [shards(): from_plus = lax.ppermute(down, 'gx', back)]
    ppermute x2, starting transfers between devices: 7.26 us -> 6.19 us  [shards(): lax.ppermute(x, 'gy', crossing)]
    ppermute x2, waiting for transfers between devices: 0.85 us -> 1.92 us  [shards(): lax.ppermute(x, 'gy', crossing)]
  transfers between devices with their start and end apart: 15 -> 15, of which waited for: 4 -> 5; matrix products, arithmetic and copies ran while one was open for 0% -> 0% of each run, Pallas kernels for 12% -> 11%
where the time goes in v3:
time: 66.6 us; the launch traced here: 66.5 us
  Pallas kernels  27.8 us (42%)
  starting transfers between devices  25 us (38%)
  waiting for transfers between devices  12.9 us (19%)
  between operations  0.78 us (1%)
    pallas_call x1, Pallas kernels, shards(): pl.pallas_call(density_kernel, out_shape=[struct((CODES * G, 128)), folde...  17.6 us
    pallas_call x1, Pallas kernels, shards(): pl.pallas_call(root_kernel, out_shape=[struct((DIM, DIM)), struct((DIM, D...  6.25 us
    ppermute x2, starting transfers between devices, shards(): lax.ppermute(x, 'gy', crossing)  6.19 us
    ppermute x2, starting transfers between devices, shards(): minus.append(lax.ppermute(up, 'gx', ahead))  5.73 us
    ppermute x1, starting transfers between devices, shards(): side = lax.ppermute(side, 'gy', crossing)  4.63 us
    ppermute x1, waiting for transfers between devices, shards(): x = lax.ppermute(x, 'gy', crossing)  3.74 us
    ppermute x1, waiting for transfers between devices, shards(): from_plus = lax.ppermute(down, 'gx', back)  3.62 us
    ppermute x1, starting transfers between devices, shards(): x = lax.ppermute(x, 'gy', crossing)  3.58 us
  transfers between devices with their start and end apart: 15, of which 5 were waited for; matrix products, arithmetic and copies ran while one was open for 0% of the time, Pallas kernels for 11%

profile of v3, /device:TPU:24, one launch (start us, length us, event | category | flops | bytes accessed | tf_op | source)
XLA Modules:
  0.0 66.5 jit_solution(3255443458814163095)
XLA Ops:
  0.0 1.2 %pack0.1 = (f32[104,512]{1,0:T(8,128)S(1)}, f32[104,512]{1,0:T(8,128)S(1)}, f32[96,896]{1,0:T(8,128)S(1)}, f32[23,4,828]{2,1,0:T(4,128)S(1)}) custom-call(f32[2,23,4,828]{3,2,1,0:T(4,128)} %bitcast.8), custom_call_target="tpu_custom_call" | custom-call | tf_op jit(solution)/shard_map/pack0/pallas_call | solution.py:415
  1.2 0.1 pack1.1
  1.3 0.8 %collective-permute-start = (f32[96,640]{1,0:T(8,128)S(1)}, f32[96,640]{1,0:T(8,128)S(1)}, u32[]{:S(2)}, u32[]{:S(2)}) collective-permute-start(f32[96,640]{1,0:T(8,128)S(1)} %get-tuple-element.29), channel_id=1, source_target_pairs={{32,0},{64,32},{96,64},{0,96},{33,1},{65,33},{97,65},{1,97},{34,2}... | collective-permute-start | bytes 737288 | tf_op jit(solution)/shard_map/ppermute | solution.py:435
  2.1 2.5 %collective-permute-start.1 = (f32[96,640]{1,0:T(8,128)S(1)}, f32[96,640]{1,0:T(8,128)S(1)}, u32[]{:S(2)}, u32[]{:S(2)}) collective-permute-start(f32[96,640]{1,0:T(8,128)S(1)} %get-tuple-element.30), channel_id=1, source_target_pairs={{0,32},{32,64},{64,96},{96,0},{1,33},{33,65},{65,97},{97,1},{2,34}... | collective-permute-start | bytes 737288 | tf_op jit(solution)/shard_map/ppermute | solution.py:436
  4.6 0.0 collective-permute-start.6
  4.6 3.2 %collective-permute-start.7 = (f32[104,512]{1,0:T(8,128)S(1)}, f32[104,512]{1,0:T(8,128)S(1)}, u32[]{:S(2)}, u32[]{:S(2)}) collective-permute-start(f32[104,512]{1,0:T(8,128)S(1)} %get-tuple-element.36), channel_id=1, source_target_pairs={{0,32},{32,64},{64,96},{96,0},{1,33},{33,65},{65,97},{97,1},{2,34}... | collective-permute-start | bytes 638984 | tf_op jit(solution)/shard_map/ppermute | solution.py:436
  7.9 0.3 side.1
  8.2 4.6 %collective-permute-start.2 = (f32[96,1152]{1,0:T(8,128)S(1)}, f32[96,1152]{1,0:T(8,128)S(1)}, u32[]{:S(2)}, u32[]{:S(2)}) collective-permute-start(f32[96,1152]{1,0:T(8,128)S(1)} %side.1), channel_id=1, source_target_pairs={{0,31},{1,2},{2,1},{3,4},{4,3},{5,6},{6,5},{7,8},{8,7},{9,10},{10,... | collective-permute-start | bytes 1327112 | tf_op jit(solution)/shard_map/ppermute | solution.py:446
  13.5 0.1 pad_add_fusion.codes_ref
  13.6 1.3 %collective-permute-done.6.plus_ref = f32[104,512]{1,0:T(8,128)S(1)} collective-permute-done((f32[104,512]{1,0:T(8,128)S(1)}, f32[104,512]{1,0:T(8,128)S(1)}, u32[]{:S(2)}, u32[]{:S(2)}) %collective-permute-start.6) | collective-permute-done | bytes 213024 | tf_op jit(solution)/shard_map/ppermute | solution.py:435
  14.9 0.0 collective-permute-done.7.minus_ref
  14.9 0.4 corner0.1
  15.3 4.9 %collective-permute-start.8 = (f32[96,768]{1,0:T(8,128)S(1)}, f32[96,768]{1,0:T(8,128)S(1)}, u32[]{:S(2)}, u32[]{:S(2)}) collective-permute-start(f32[96,768]{1,0:T(8,128)S(1)} %get-tuple-element.37), channel_id=1, source_target_pairs={{0,31},{1,2},{2,1},{3,4},{4,3},{5,6},{6,5},{7,8},{8,7},{9,10},{10,... | collective-permute-start | bytes 884744 | tf_op jit(solution)/shard_map/ppermute | solution.py:459
  20.2 0.0 collective-permute-start.9
  20.2 0.0 collective-permute-done.plus_ref
  20.2 0.5 collective-permute-start.10
  20.7 0.0 collective-permute-done.1.minus_ref
  20.7 0.4 corner1.1
  21.1 1.3 %collective-permute-start.3 = (f32[96,768]{1,0:T(8,128)S(1)}, f32[96,768]{1,0:T(8,128)S(1)}, u32[]{:S(2)}, u32[]{:S(2)}) collective-permute-start(f32[96,768]{1,0:T(8,128)S(1)} %get-tuple-element.32), channel_id=1, source_target_pairs={{0,31},{1,2},{2,1},{3,4},{4,3},{5,6},{6,5},{7,8},{8,7},{9,10},{10,... | collective-permute-start | bytes 884744 | tf_op jit(solution)/shard_map/ppermute | solution.py:459
  22.4 0.0 collective-permute-start.4
  22.4 0.5 collective-permute-start.5
  22.9 1.9 %collective-permute-done.8.cross_ref = f32[96,768]{1,0:T(8,128)S(1)} collective-permute-done((f32[96,768]{1,0:T(8,128)S(1)}, f32[96,768]{1,0:T(8,128)S(1)}, u32[]{:S(2)}, u32[]{:S(2)}) %collective-permute-start.8) | collective-permute-done | bytes 294944 | tf_op jit(solution)/shard_map/ppermute | solution.py:459
  24.8 6.2 %inverse_root.1 = (f32[768,768]{1,0:T(8,128)S(1)}, bf16[768,768]{1,0:T(8,128)(2,1)S(1)}, bf16[768,768]{1,0:T(8,128)(2,1)S(1)}) custom-call(s32[1]{0:T(128)} %bitcast.odd_ref, s32[32]{0:T(128)S(1)} %pad_add_fusion.codes_ref, f32[96,896]{1,0:T(8,128)S(1)} %get-tuple-element.31.margin_ref.own_ref, f32[104,512]{1,0:T(8,128)S(1)} %collective-permute-done.6.plus_ref, ...), custom_call_target="tpu_custom_call" | custom-call | flops 3623878656 | bytes 8388608 | tf_op jit(solution)/shard_map/inverse_root/pallas_call | solution.py:467
  31.1 17.6 %density.1 = (f32[864,128]{1,0:T(8,128)S(1)}, f32[104,256]{1,0:T(8,128)S(1)}, f32[96,276]{1,0:T(8,128)S(1)}, f32[104,256]{1,0:T(8,128)S(1)}) custom-call(s32[1]{0:T(128)} %bitcast.odd_ref, s32[32]{0:T(128)S(1)} %pad_add_fusion.codes_ref, f32[1]{0:T(128)S(6)} %copy.4.chem_ref, f32[96,896]{1,0:T(8,128)S(1)} %get-tuple-element.28.ham_ref.own_ref, ...), custom_call_target="tpu_custom_call" | custom-call | flops 10871635968 | bytes 8388608 | tf_op jit(solution)/shard_map/density/pallas_call | solution.py:478
  48.8 3.0 %collective-permute-start.11 = (f32[104,256]{1,0:T(8,128)S(1)}, f32[104,256]{1,0:T(8,128)S(1)}, u32[]{:S(2)}, u32[]{:S(2)}) collective-permute-start(f32[104,256]{1,0:T(8,128)S(1)} %get-tuple-element.45), channel_id=1, source_target_pairs={{0,32},{32,64},{64,96},{96,0},{1,33},{33,65},{65,97},{97,1},{2,34}... | collective-permute-start | bytes 319496 | tf_op jit(solution)/shard_map/ppermute | solution.py:490
  51.8 2.3 %collective-permute-done.11.up_ref = f32[104,256]{1,0:T(8,128)S(1)} collective-permute-done((f32[104,256]{1,0:T(8,128)S(1)}, f32[104,256]{1,0:T(8,128)S(1)}, u32[]{:S(2)}, u32[]{:S(2)}) %collective-permute-start.11) | collective-permute-done | bytes 106528 | tf_op jit(solution)/shard_map/ppermute | solution.py:490
  54.1 3.6 %collective-permute-done.12.down_ref = f32[104,256]{1,0:T(8,128)S(1)} collective-permute-done((f32[104,256]{1,0:T(8,128)S(1)}, f32[104,256]{1,0:T(8,128)S(1)}, u32[]{:S(2)}, u32[]{:S(2)}) %collective-permute-start.12) | collective-permute-done | bytes 106528 | tf_op jit(solution)/shard_map/ppermute | solution.py:491
  57.7 0.2 turn.1
  57.9 3.6 %collective-permute-start.13 = (f32[104,256]{1,0:T(8,128)S(1)}, f32[104,256]{1,0:T(8,128)S(1)}, u32[]{:S(2)}, u32[]{:S(2)}) collective-permute-start(f32[104,256]{1,0:T(8,128)S(1)} %get-tuple-element.47), channel_id=1, source_target_pairs={{0,31},{1,2},{2,1},{3,4},{4,3},{5,6},{6,5},{7,8},{8,7},{9,10},{10,... | collective-permute-start | bytes 319496 | tf_op jit(solution)/shard_map/ppermute | solution.py:509
  61.5 0.2 own.1.w_ref
  61.7 3.7 %collective-permute-done.13.cross_ref = f32[104,256]{1,0:T(8,128)S(1)} collective-permute-done((f32[104,256]{1,0:T(8,128)S(1)}, f32[104,256]{1,0:T(8,128)S(1)}, u32[]{:S(2)}, u32[]{:S(2)}) %collective-permute-start.13) | collective-permute-done | bytes 106528 | tf_op jit(solution)/shard_map/ppermute | solution.py:509
  65.5 1.0 %symmetrize.1 = f32[23,4,828]{2,1,0:T(4,128)} custom-call(s32[1]{0:T(128)} %bitcast.odd_ref, f32[7,96,128]{2,1,0:T(8,128)S(1)} %own.1.w_ref, f32[96,276]{1,0:T(8,128)S(1)} %get-tuple-element.44.mid_ref, f32[104,256]{1,0:T(8,128)S(1)} %collective-permute-done.11.up_ref, f32[104,256]{1,0:T(8,128)S(1)} %collective-permute-done.12.down_ref, ...), custom_call_target="tpu_custom_call" | custom-call | tf_op jit(solution)/shard_map/symmetrize/pallas_call | solution.py:511
  (12 shorter events, 0.0 us)
Async XLA Ops:
  0.0 13.5 %copy-start = (s32[1,1,28]{2,1,0:T(1,128)S(1)}, s32[1,1,28]{2,1,0:T(1,128)}, u32[]{:S(2)}) copy-start(s32[1,1,28]{2,1,0:T(1,128)} %param.4) | copy-start | bytes 340
  1.3 18.9 %collective-permute-start = (f32[96,640]{1,0:T(8,128)S(1)}, f32[96,640]{1,0:T(8,128)S(1)}, u32[]{:S(2)}, u32[]{:S(2)}) collective-permute-start(f32[96,640]{1,0:T(8,128)S(1)} %get-tuple-element.29), channel_id=1, source_target_pairs={{32,0},{64,32},{96,64},{0,96},{33,1},{65,33},{97,65},{1,97},{34,2}... | collective-permute-start | bytes 737288 | tf_op jit(solution)/shard_map/ppermute | solution.py:435
  2.1 18.5 %collective-permute-start.1 = (f32[96,640]{1,0:T(8,128)S(1)}, f32[96,640]{1,0:T(8,128)S(1)}, u32[]{:S(2)}, u32[]{:S(2)}) collective-permute-start(f32[96,640]{1,0:T(8,128)S(1)} %get-tuple-element.30), channel_id=1, source_target_pairs={{0,32},{32,64},{64,96},{96,0},{1,33},{33,65},{65,97},{97,1},{2,34}... | collective-permute-start | bytes 737288 | tf_op jit(solution)/shard_map/ppermute | solution.py:436
  4.6 10.2 %collective-permute-start.6 = (f32[104,512]{1,0:T(8,128)S(1)}, f32[104,512]{1,0:T(8,128)S(1)}, u32[]{:S(2)}, u32[]{:S(2)}) collective-permute-start(f32[104,512]{1,0:T(8,128)S(1)} %get-tuple-element.35), channel_id=1, source_target_pairs={{32,0},{64,32},{96,64},{0,96},{33,1},{65,33},{97,65},{1,97},{34,2}... | collective-permute-start | bytes 638984 | tf_op jit(solution)/shard_map/ppermute | solution.py:435
  4.6 10.2 %collective-permute-start.7 = (f32[104,512]{1,0:T(8,128)S(1)}, f32[104,512]{1,0:T(8,128)S(1)}, u32[]{:S(2)}, u32[]{:S(2)}) collective-permute-start(f32[104,512]{1,0:T(8,128)S(1)} %get-tuple-element.36), channel_id=1, source_target_pairs={{0,32},{32,64},{64,96},{96,0},{1,33},{33,65},{65,97},{97,1},{2,34}... | collective-permute-start | bytes 638984 | tf_op jit(solution)/shard_map/ppermute | solution.py:436
  8.2 14.2 %collective-permute-start.2 = (f32[96,1152]{1,0:T(8,128)S(1)}, f32[96,1152]{1,0:T(8,128)S(1)}, u32[]{:S(2)}, u32[]{:S(2)}) collective-permute-start(f32[96,1152]{1,0:T(8,128)S(1)} %side.1), channel_id=1, source_target_pairs={{0,31},{1,2},{2,1},{3,4},{4,3},{5,6},{6,5},{7,8},{8,7},{9,10},{10,... | collective-permute-start | bytes 1327112 | tf_op jit(solution)/shard_map/ppermute | solution.py:446
  15.3 9.5 %collective-permute-start.8 = (f32[96,768]{1,0:T(8,128)S(1)}, f32[96,768]{1,0:T(8,128)S(1)}, u32[]{:S(2)}, u32[]{:S(2)}) collective-permute-start(f32[96,768]{1,0:T(8,128)S(1)} %get-tuple-element.37), channel_id=1, source_target_pairs={{0,31},{1,2},{2,1},{3,4},{4,3},{5,6},{6,5},{7,8},{8,7},{9,10},{10,... | collective-permute-start | bytes 884744 | tf_op jit(solution)/shard_map/ppermute | solution.py:459
  20.2 4.7 %collective-permute-start.9 = (f32[96,768]{1,0:T(8,128)S(1)}, f32[96,768]{1,0:T(8,128)S(1)}, u32[]{:S(2)}, u32[]{:S(2)}) collective-permute-start(f32[96,768]{1,0:T(8,128)S(1)} %get-tuple-element.38), channel_id=1, source_target_pairs={{0,1},{1,0},{2,3},{3,2},{4,5},{5,4},{6,7},{7,6},{8,9},{9,8},{10,11... | collective-permute-start | bytes 884744 | tf_op jit(solution)/shard_map/ppermute | solution.py:459
  20.2 2.2 %collective-permute-start.10 = (f32[96,640]{1,0:T(8,128)S(1)}, f32[96,640]{1,0:T(8,128)S(1)}, u32[]{:S(2)}, u32[]{:S(2)}) collective-permute-start(f32[96,640]{1,0:T(8,128)S(1)} %get-tuple-element.39), channel_id=1, source_target_pairs={{0,1},{1,0},{2,3},{3,2},{4,5},{5,4},{6,7},{7,6},{8,9},{9,8},{10,11... | collective-permute-start | bytes 737288 | tf_op jit(solution)/shard_map/ppermute | solution.py:459
  21.1 10.0 %collective-permute-start.3 = (f32[96,768]{1,0:T(8,128)S(1)}, f32[96,768]{1,0:T(8,128)S(1)}, u32[]{:S(2)}, u32[]{:S(2)}) collective-permute-start(f32[96,768]{1,0:T(8,128)S(1)} %get-tuple-element.32), channel_id=1, source_target_pairs={{0,31},{1,2},{2,1},{3,4},{4,3},{5,6},{6,5},{7,8},{8,7},{9,10},{10,... | collective-permute-start | bytes 884744 | tf_op jit(solution)/shard_map/ppermute | solution.py:459
  22.4 8.7 %collective-permute-start.4 = (f32[96,768]{1,0:T(8,128)S(1)}, f32[96,768]{1,0:T(8,128)S(1)}, u32[]{:S(2)}, u32[]{:S(2)}) collective-permute-start(f32[96,768]{1,0:T(8,128)S(1)} %get-tuple-element.33), channel_id=1, source_target_pairs={{0,1},{1,0},{2,3},{3,2},{4,5},{5,4},{6,7},{7,6},{8,9},{9,8},{10,11... | collective-permute-start | bytes 884744 | tf_op jit(solution)/shard_map/ppermute | solution.py:459
  22.4 8.7 %collective-permute-start.5 = (f32[96,640]{1,0:T(8,128)S(1)}, f32[96,640]{1,0:T(8,128)S(1)}, u32[]{:S(2)}, u32[]{:S(2)}) collective-permute-start(f32[96,640]{1,0:T(8,128)S(1)} %get-tuple-element.34), channel_id=1, source_target_pairs={{0,1},{1,0},{2,3},{3,2},{4,5},{5,4},{6,7},{7,6},{8,9},{9,8},{10,11... | collective-permute-start | bytes 737288 | tf_op jit(solution)/shard_map/ppermute | solution.py:459
  48.8 5.3 %collective-permute-start.11 = (f32[104,256]{1,0:T(8,128)S(1)}, f32[104,256]{1,0:T(8,128)S(1)}, u32[]{:S(2)}, u32[]{:S(2)}) collective-permute-start(f32[104,256]{1,0:T(8,128)S(1)} %get-tuple-element.45), channel_id=1, source_target_pairs={{0,32},{32,64},{64,96},{96,0},{1,33},{33,65},{65,97},{97,1},{2,34}... | collective-permute-start | bytes 319496 | tf_op jit(solution)/shard_map/ppermute | solution.py:490
  51.8 5.9 %collective-permute-start.12 = (f32[104,256]{1,0:T(8,128)S(1)}, f32[104,256]{1,0:T(8,128)S(1)}, u32[]{:S(2)}, u32[]{:S(2)}) collective-permute-start(f32[104,256]{1,0:T(8,128)S(1)} %get-tuple-element.46), channel_id=1, source_target_pairs={{32,0},{64,32},{96,64},{0,96},{33,1},{65,33},{97,65},{1,97},{34,2}... | collective-permute-start | bytes 319496 | tf_op jit(solution)/shard_map/ppermute | solution.py:491
  57.9 7.5 %collective-permute-start.13 = (f32[104,256]{1,0:T(8,128)S(1)}, f32[104,256]{1,0:T(8,128)S(1)}, u32[]{:S(2)}, u32[]{:S(2)}) collective-permute-start(f32[104,256]{1,0:T(8,128)S(1)} %get-tuple-element.47), channel_id=1, source_target_pairs={{0,31},{1,2},{2,1},{3,4},{4,3},{5,6},{6,5},{7,8},{8,7},{9,10},{10,... | collective-permute-start | bytes 319496 | tf_op jit(solution)/shard_map/ppermute | solution.py:509
  61.5 4.0 %collective-permute-start.14 = (f32[104,256]{1,0:T(8,128)S(1)}, f32[104,256]{1,0:T(8,128)S(1)}, u32[]{:S(2)}, u32[]{:S(2)}) collective-permute-start(f32[104,256]{1,0:T(8,128)S(1)} %get-tuple-element.48), channel_id=1, source_target_pairs={{0,1},{1,0},{2,3},{3,2},{4,5},{5,4},{6,7},{7,6},{8,9},{9,8},{10,11... | collective-permute-start | bytes 319496 | tf_op jit(solution)/shard_map/ppermute | solution.py:510
